TPU v7x, 32 devices: a whole 2x2x4 slice. The times are simulated.
32 devices in a mesh: unit: 8 (over z, y), dp: 4 (over x, core).
Axes of the slice: x: 2, y: 2, z: 4, core: 2. Of those that a mesh axis runs over, the one named last changes fastest.
Arguments:
- token_ids: int32 [4, 8, 512], P('dp'), may hold values from 0 to 30719
- segments: int32 [4, 8, 512], P('dp', 'unit'), may hold values from 0 to 7, never falling along the last dimension, each value on 1 to 256 neighbouring positions
- positions: int32 [4, 8, 64], P('dp', 'unit'), may hold values from 0 to 511
- teacher: bfloat16 [4, 8, 64, 30720], P('dp', None, None, 'unit'), may hold values from -18 to 18, as said below
- gate_noise: float32 [782], replicated, may hold values from 0.01 to 0.99
- unit_noise: float32 [3072], replicated, may hold values from 0.01 to 0.99
- multipliers: float32 [2], replicated, may hold values from 2 to 40
- step_count: int32 [1], replicated, may hold values from 1 to 20
- layer_mats: float32 [768, 4352], P(('unit', 'dp')), as said below
- mats_first: float32 [768, 4352], P(('unit', 'dp')), may hold values from -9.536743e-07 to 9.536743e-07
- mats_second: float32 [768, 4352], P(('unit', 'dp')), may hold values from 3.1512686e-13 to 1.2605074e-12
- layer_vecs: float32 [14, 768], P(None, ('unit', 'dp')), as said below
- vecs_first: float32 [14, 768], P(None, ('unit', 'dp')), may hold values from -9.536743e-07 to 9.536743e-07
- vecs_second: float32 [14, 768], P(None, ('unit', 'dp')), may hold values from 3.1512686e-13 to 1.2605074e-12
- ffn_mats: float32 [2, 768, 3072], P(None, 'dp', 'unit'), as said below
- ffn_first: float32 [2, 768, 3072], P(None, 'dp', 'unit'), may hold values from -9.536743e-07 to 9.536743e-07
- ffn_second: float32 [2, 768, 3072], P(None, 'dp', 'unit'), may hold values from 3.1512686e-13 to 1.2605074e-12
- unit_vecs: float32 [2, 3072], P(None, ('unit', 'dp')), as said below
- unit_first: float32 [2, 3072], P(None, ('unit', 'dp')), may hold values from -9.536743e-07 to 9.536743e-07
- unit_second: float32 [2, 3072], P(None, ('unit', 'dp')), may hold values from 3.1512686e-13 to 1.2605074e-12
- word_table: float32 [30720, 768], P('unit', 'dp'), may hold values from -0.6 to 0.6, as said below
- table_first: float32 [30720, 768], P('unit', 'dp'), may hold values from -9.536743e-07 to 9.536743e-07
- table_second: float32 [30720, 768], P('unit', 'dp'), may hold values from 3.1512686e-13 to 1.2605074e-12
- word_bias: float32 [30720], P(('unit', 'dp')), may hold values from -3 to 3
- bias_first: float32 [30720], P(('unit', 'dp')), may hold values from -9.536743e-07 to 9.536743e-07
- bias_second: float32 [30720], P(('unit', 'dp')), may hold values from 3.1512686e-13 to 1.2605074e-12
- mask_logits: float32 [14], replicated, may hold values from 3 to 6
- mask_first: float32 [14], replicated, may hold values from -9.536743e-07 to 9.536743e-07
- mask_second: float32 [14], replicated, may hold values from 3.1512686e-13 to 1.2605074e-12
Outputs:
- loss: float32 [], replicated
- kept: float32 [], replicated
- grad_norm: float32 [], replicated
- mats_new: float32 [768, 4352], P(('unit', 'dp'))
- mats_grad: float32 [768, 4352], P(('unit', 'dp'))
- vecs_new: float32 [14, 768], P(None, ('unit', 'dp'))
- vecs_grad: float32 [14, 768], P(None, ('unit', 'dp'))
- ffn_new: float32 [2, 768, 3072], P(None, 'dp', 'unit')
- ffn_grad: float32 [2, 768, 3072], P(None, 'dp', 'unit')
- unit_new: float32 [2, 3072], P(None, ('unit', 'dp'))
- unit_grad: float32 [2, 3072], P(None, ('unit', 'dp'))
- table_new: float32 [30720, 768], P('unit', 'dp')
- table_grad: float32 [30720, 768], P('unit', 'dp')
- bias_new: float32 [30720], P(('unit', 'dp'))
- bias_grad: float32 [30720], P(('unit', 'dp'))
- mask_new: float32 [14], replicated
- mask_grad: float32 [14], replicated
Inputs may be any that keep to these rules, and one draw needn't show every extreme that they name: `token_ids`: token ids index the vocabulary. `segments`: segment numbers never fall along a row. Masked positions index tokens of their row; they may repeat. layer_mats entries are independent normal draws. layer_vecs: gains near one, biases of either sign, hidden logits. ffn_mats entries are independent normal draws. unit_vecs: biases of either sign and unit logits. teacher logits are independent draws. word_table entries are independent draws.
All inputs are finite; a program needn't handle non-finite values.
Results may differ from a plain program's by a relative error of at most 0.012.
The roundings to bfloat16 on the way count: a program that leaves them out, or rounds other values in their place, can miss the bound.
Values may be sent and summed in bfloat16 or wider, within the bound.
A program may use at most 320 MiB of HBM per device.

v0:
```python
import math

import jax
import jax.numpy as jnp
from jax import lax
from jax.sharding import PartitionSpec as P

EPS_NORM = 1e-12
GAMMA = -0.1
ZETA = 1.1
BETA = 2.0 / 3.0
TARGET = 0.95
TEMPER = 2.0
MAX_NORM = 0.0001
BETA_ONE = 0.9
BETA_TWO = 0.999
ADAM_EPS = 1e-08
DECAY = 0.01
RATE_MATS = 0.5
RATE_VECS = 5.0
RATE_TABLE = 1.0


def joined(array, axis, combine):
    everything = jax.tree.map(
        lambda part, kind: lax.all_gather(part.astype(kind), axis),
        array,
        (jnp.bfloat16, jnp.bfloat16, jnp.bfloat16, jnp.bfloat16, jnp.bfloat16, jnp.bfloat16),
    )

    def take(k):
        return jax.tree.map(lambda part, own: part[k].astype(own.dtype), everything, array)

    return lax.fori_loop(
        1, lax.axis_size(axis), lambda k, so_far: combine(so_far, take(k)), take(0)
    )


def rounded(values):
    return lax.optimization_barrier(values.astype(jnp.bfloat16)).astype(jnp.float32)


def layer_norm(values, gain, shift):
    center = values - jnp.mean(values, -1, keepdims=True)
    spread = jnp.mean(center * center, -1, keepdims=True)
    return center * lax.rsqrt(spread + EPS_NORM) * gain + shift


def norm_back(values, gain, shift, grad):
    _, pull = jax.vjp(layer_norm, values, gain, shift)
    return pull(grad)


def gelu_back(values, grad):
    _, pull = jax.vjp(jax.nn.gelu, values)
    return pull(grad)[0]


def gate(logit, noise):
    soft = jax.nn.sigmoid((jnp.log(noise) - jnp.log(1.0 - noise) + logit) / BETA)
    return jnp.clip(soft * (ZETA - GAMMA) + GAMMA, 0.0, 1.0)


def gate_back(logit, noise, grad):
    _, pull = jax.vjp(gate, logit, noise)
    return pull(grad)[0]


def keep_score(logit):
    return jax.nn.sigmoid(logit - BETA * math.log(-GAMMA / ZETA))


def score_slope(logit):
    score = keep_score(logit)
    return score * (1.0 - score)


def contract_rows(left, right):
    return lax.dot_general(
        left, right, (((0,), (0,)), ((), ())), preferred_element_type=jnp.float32
    )


def head_probs(queries, keys_b, segment, heads):
    length, width = queries.shape
    shape3 = (length, heads, width // heads)
    scores = jnp.einsum(
        "qhd,khd->hqk",
        queries.reshape(shape3),
        keys_b.reshape(shape3),
        preferred_element_type=jnp.float32,
    ) * (width // heads) ** (-0.5)
    same = segment[:, None] == segment[None, :]
    return jax.nn.softmax(jnp.where(same[None], scores, -1000000000.0), axis=-1)


def attend(queries, keys_b, values_b, segment, heads):
    length, width = queries.shape
    probs = head_probs(queries, keys_b, segment, heads)
    context = jnp.einsum(
        "hqk,khd->qhd",
        probs.astype(jnp.bfloat16),
        values_b.reshape(length, heads, width // heads),
        preferred_element_type=jnp.float32,
    )
    return context.reshape(length, width)


def attend_back(queries, keys_b, values_b, segment, grad_ctx, heads):
    length, width = queries.shape
    shape3 = (length, heads, width // heads)
    scale = (width // heads) ** (-0.5)
    probs = head_probs(queries, keys_b, segment, heads)
    grad_heads = grad_ctx.reshape(shape3)
    grad_probs = jnp.einsum(
        "qhd,khd->hqk", grad_heads, values_b.reshape(shape3), preferred_element_type=jnp.float32
    )
    grad_scores = (probs * (grad_probs - jnp.sum(grad_probs * probs, -1, keepdims=True))).astype(
        jnp.bfloat16
    )
    grad_q = (
        jnp.einsum(
            "hqk,khd->qhd", grad_scores, keys_b.reshape(shape3), preferred_element_type=jnp.float32
        )
        * scale
    )
    grad_k = (
        jnp.einsum(
            "hqk,qhd->khd", grad_scores, queries.reshape(shape3), preferred_element_type=jnp.float32
        )
        * scale
    )
    grad_v = jnp.einsum(
        "hqk,qhd->khd", probs.astype(jnp.bfloat16), grad_heads, preferred_element_type=jnp.float32
    )
    return (
        grad_q.reshape(length, width),
        grad_k.reshape(length, width),
        grad_v.reshape(length, width),
    )


def merge_stats(first, second):
    s_max = jnp.maximum(first[0], second[0])
    s_sum = first[1] * jnp.exp(first[0] - s_max) + second[1] * jnp.exp(second[0] - s_max)
    t_max = jnp.maximum(first[2], second[2])
    left = jnp.exp(first[2] - t_max)
    right = jnp.exp(second[2] - t_max)
    return (
        s_max,
        s_sum,
        t_max,
        first[3] * left + second[3] * right,
        first[4] * left + second[4] * right,
        first[5] + second[5],
    )


def adamw(weight, first, second, grad, rate, count):
    first = BETA_ONE * first + (1.0 - BETA_ONE) * grad
    second = BETA_TWO * second + (1.0 - BETA_TWO) * grad * grad
    first_hat = first / (1.0 - BETA_ONE**count)
    second_hat = second / (1.0 - BETA_TWO**count)
    return weight - rate * (first_hat / (jnp.sqrt(second_hat) + ADAM_EPS) + DECAY * weight)


def on_device(
    token_ids,
    segments,
    positions,
    teacher,
    gate_noise,
    unit_noise,
    multipliers,
    step_count,
    layer_mats,
    mats_first,
    mats_second,
    layer_vecs,
    vecs_first,
    vecs_second,
    ffn_mats,
    ffn_first,
    ffn_second,
    unit_vecs,
    unit_first,
    unit_second,
    word_table,
    table_first,
    table_second,
    word_bias,
    bias_first,
    bias_second,
    mask_logits,
    mask_first,
    mask_second,
):
    low_type = jnp.bfloat16
    full_type = jnp.float32
    units_n = lax.axis_size("unit")
    groups_n = lax.axis_size("dp")
    heads = mask_logits.shape[0] - 2
    mats_all, vecs_all = (
        lax.all_gather(layer_mats.astype(low_type), ("unit", "dp"), axis=0, tiled=True),
        lax.all_gather(layer_vecs.astype(low_type), ("unit", "dp"), axis=1, tiled=True),
    )
    ffn_group, unit_group, table_group, bias_group = (
        lax.all_gather(ffn_mats.astype(low_type), "dp", axis=1, tiled=True),
        lax.all_gather(unit_vecs.astype(low_type), "dp", axis=1, tiled=True),
        lax.all_gather(word_table.astype(low_type), "dp", axis=1, tiled=True),
        lax.all_gather(word_bias.astype(low_type), "dp", axis=0, tiled=True),
    )
    width = mats_all.shape[0]
    head_size = width // heads
    rows_dev = segments.shape[1]
    seq_len = segments.shape[2]
    tokens_dev = rows_dev * seq_len
    vecs_f = vecs_all.astype(full_type)
    masks_r = rounded(mask_logits)
    hid_logit = vecs_f[13]
    noise_hid = gate_noise[:width]
    noise_head = gate_noise[width : width + heads]
    zhid = gate(hid_logit, noise_hid)
    zhead = gate(masks_r[:heads], noise_head)
    zmha = gate(masks_r[heads], gate_noise[width + heads])
    zmlp = gate(masks_r[heads + 1], gate_noise[width + heads + 1])
    unit_idx = lax.axis_index("unit")
    slice_units = unit_group.shape[1]
    ffn_width = slice_units * units_n
    group_ids = token_ids.reshape(-1)
    vocab_slice = table_group.shape[0]
    base_row = unit_idx * vocab_slice
    local = group_ids - base_row
    inside = (local >= 0) & (local < vocab_slice)
    found = jnp.take(table_group, jnp.clip(local, 0, vocab_slice - 1), axis=0)
    word = lax.psum_scatter(
        jnp.where(inside[:, None], found.astype(full_type), 0.0).astype(jnp.bfloat16),
        "unit",
        scatter_dimension=0,
        tiled=True,
    ).astype(jnp.float32)
    pos_table = mats_all[:, 5 * width : 5 * width + seq_len].astype(full_type)
    embed = (word.reshape(rows_dev, seq_len, width) + pos_table.T[None]).reshape(tokens_dev, width)
    start_norm = layer_norm(embed, vecs_f[0], vecs_f[1])
    start = start_norm * zhid
    start_low = start.astype(low_type)
    w_qkv = mats_all[:, : 3 * width]
    w_out = mats_all[:, 3 * width : 4 * width]
    w_trans = mats_all[:, 4 * width : 5 * width]
    qkv = jnp.dot(start_low, w_qkv, preferred_element_type=full_type)
    queries = (qkv[:, :width] + vecs_f[2]).astype(low_type)
    keys_b = qkv[:, width : 2 * width].astype(low_type)
    values_b = (qkv[:, 2 * width :] + vecs_f[3]).astype(low_type)
    seg_rows = segments[0]
    row_shape = (rows_dev, seq_len, width)

    def attend_row(items):
        return attend(items[0], items[1], items[2], items[3], heads)

    context = lax.map(
        attend_row,
        (
            queries.reshape(row_shape),
            keys_b.reshape(row_shape),
            values_b.reshape(row_shape),
            seg_rows,
        ),
    ).reshape(tokens_dev, width)
    context_r = rounded(context)
    zcols = jnp.repeat(zhead, head_size)
    scaled = (context_r * zcols).astype(low_type)
    attn_res = jnp.dot(scaled, w_out, preferred_element_type=full_type) + vecs_f[4]
    middle_in = start + attn_res * zmha * zhid
    middle = layer_norm(middle_in, vecs_f[5], vecs_f[6])
    middle_low = middle.astype(low_type)
    rows_all = lax.all_gather(middle_low, "unit", axis=0, tiled=True)
    up_w = ffn_group[0]
    down_w = ffn_group[1]
    unit_bias = unit_group[0].astype(full_type)
    unit_logit = unit_group[1].astype(full_type)
    noise_units = lax.dynamic_slice_in_dim(unit_noise, unit_idx * slice_units, slice_units, 0)
    zunit = gate(unit_logit, noise_units)
    hidden_pre = jnp.dot(rows_all, up_w, preferred_element_type=full_type) + unit_bias
    hidden_gelu = jax.nn.gelu(hidden_pre)
    hidden = (hidden_gelu * zunit).astype(low_type)
    ffn_out = lax.psum_scatter(
        jnp.dot(hidden, down_w.T, preferred_element_type=full_type).astype(jnp.bfloat16),
        "unit",
        scatter_dimension=0,
        tiled=True,
    ).astype(jnp.float32)
    ffn_res = ffn_out + vecs_f[7]
    final_in = middle + ffn_res * zmlp * zhid
    final = layer_norm(final_in, vecs_f[8], vecs_f[9])
    nmask = positions.shape[2]
    picks = (positions[0] + jnp.arange(rows_dev, dtype=jnp.int32)[:, None] * seq_len).reshape(-1)
    picked = final[picks].astype(low_type)
    trans_pre = jnp.dot(picked, w_trans, preferred_element_type=full_type) + vecs_f[10]
    trans_gelu = jax.nn.gelu(trans_pre)
    trans_low = layer_norm(trans_gelu, vecs_f[11], vecs_f[12]).astype(low_type)
    trans_all = lax.all_gather(trans_low, "unit", axis=0, tiled=True)
    student = (
        jnp.dot(trans_all, table_group.T, preferred_element_type=full_type)
        + bias_group.astype(full_type)
    ) / TEMPER
    teach = teacher.reshape(-1, vocab_slice).astype(full_type) / TEMPER
    s_max = jnp.max(student, -1)
    s_sum = jnp.sum(jnp.exp(student - s_max[:, None]), -1)
    t_max = jnp.max(teach, -1)
    t_exp = jnp.exp(teach - t_max[:, None])
    t_sum = jnp.sum(t_exp, -1)
    cross = jnp.sum(t_exp * (teach - student), -1)
    unit_part = jnp.sum(keep_score(unit_group[1].astype(full_type)))
    stats = joined((s_max, s_sum, t_max, t_sum, cross, unit_part), "unit", merge_stats)
    lse_student = stats[0] + jnp.log(stats[1])
    lse_teach = stats[2] + jnp.log(stats[3])
    kl_rows = stats[4] / stats[3] - lse_teach + lse_student
    own_count = rows_dev * nmask
    kl_own = jnp.sum(lax.dynamic_slice_in_dim(kl_rows, unit_idx * own_count, own_count, 0))
    npos = groups_n * kl_rows.shape[0]
    grad_logit = (
        TEMPER
        / npos
        * (jnp.exp(student - lse_student[:, None]) - jnp.exp(teach - lse_teach[:, None]))
    )
    grad_bias = jnp.sum(grad_logit, 0)
    grad_logit_low = grad_logit.astype(low_type)
    grad_table = contract_rows(grad_logit_low, trans_all)
    grad_trans = lax.psum_scatter(
        jnp.dot(grad_logit_low, table_group, preferred_element_type=full_type).astype(jnp.bfloat16),
        "unit",
        scatter_dimension=0,
        tiled=True,
    ).astype(jnp.float32)
    hid_sum = jnp.sum(keep_score(hid_logit))
    head_scores = keep_score(masks_r[:heads])
    mha_score = keep_score(masks_r[heads])
    mlp_score = keep_score(masks_r[heads + 1])
    head_sum = jnp.sum(head_scores) * mha_score
    unit_sum = stats[5] * mlp_score
    full_size = 4.0 * width * width + 2.0 * width * ffn_width
    kept = (4.0 * head_size * hid_sum * head_sum + 2.0 * hid_sum * unit_sum) / full_size
    sparsity = 1.0 - kept
    lagrange = multipliers[0] * (sparsity - TARGET) + multipliers[1] * (sparsity - TARGET) ** 2
    lag_slope = -(multipliers[0] + 2.0 * multipliers[1] * (sparsity - TARGET))
    grad_tgelu, grad_hgain, grad_hshift = norm_back(trans_gelu, vecs_f[11], vecs_f[12], grad_trans)
    grad_tpre = gelu_back(trans_pre, grad_tgelu)
    grad_tbias = jnp.sum(grad_tpre, 0)
    grad_tpre_low = grad_tpre.astype(low_type)
    grad_wtrans = contract_rows(picked, grad_tpre_low)
    grad_picked = jnp.dot(grad_tpre_low, w_trans.T, preferred_element_type=full_type)
    grad_final = jnp.zeros((tokens_dev, width), full_type).at[picks].add(grad_picked)
    grad_final_in, grad_gain2, grad_shift2 = norm_back(final_in, vecs_f[8], vecs_f[9], grad_final)
    grad_fres = grad_final_in * zmlp * zhid
    grad_dbias = jnp.sum(grad_fres, 0)
    grad_zmlp = jnp.sum(grad_final_in * ffn_res * zhid)
    grad_zhid = jnp.sum(grad_final_in * ffn_res * zmlp, 0)
    grad_fout = grad_fres.astype(low_type)
    back_all = lax.all_gather(grad_fout, "unit", axis=0, tiled=True)
    grad_hidden = jnp.dot(back_all, down_w, preferred_element_type=full_type)
    grad_down = contract_rows(back_all, hidden)
    grad_zunit = jnp.sum(grad_hidden * hidden_gelu, 0)
    grad_hpre = gelu_back(hidden_pre, grad_hidden * zunit)
    grad_ubias = jnp.sum(grad_hpre, 0)
    grad_hpre_low = grad_hpre.astype(low_type)
    grad_up = contract_rows(rows_all, grad_hpre_low)
    grad_ulogit = gate_back(unit_logit, noise_units, grad_zunit)
    grad_middle_ffn = lax.psum_scatter(
        jnp.dot(grad_hpre_low, up_w.T, preferred_element_type=full_type).astype(jnp.bfloat16),
        "unit",
        scatter_dimension=0,
        tiled=True,
    ).astype(jnp.float32)
    grad_ffn = jnp.stack([grad_up, grad_down])
    grad_unit = jnp.stack([grad_ubias, grad_ulogit])
    grad_middle_in, grad_gain1, grad_shift1 = norm_back(
        middle_in, vecs_f[5], vecs_f[6], grad_final_in + grad_middle_ffn
    )
    grad_ares = grad_middle_in * zmha * zhid
    grad_obias = jnp.sum(grad_ares, 0)
    grad_zmha = jnp.sum(grad_middle_in * attn_res * zhid)
    grad_zhid = grad_zhid + jnp.sum(grad_middle_in * attn_res * zmha, 0)
    grad_ares_low = grad_ares.astype(low_type)
    grad_wout = contract_rows(scaled, grad_ares_low)
    grad_scaled = jnp.dot(grad_ares_low, w_out.T, preferred_element_type=full_type)
    grad_zhead = jnp.sum(
        (grad_scaled * context_r).reshape(tokens_dev, heads, head_size), axis=(0, 2)
    )
    grad_context = (grad_scaled * zcols).astype(low_type)

    def back_row(items):
        return attend_back(items[0], items[1], items[2], items[3], items[4], heads)

    grad_q, grad_k, grad_v = lax.map(
        back_row,
        (
            queries.reshape(row_shape),
            keys_b.reshape(row_shape),
            values_b.reshape(row_shape),
            seg_rows,
            grad_context.reshape(row_shape),
        ),
    )
    grad_qkv = jnp.concatenate(
        [
            grad_q.reshape(tokens_dev, width),
            grad_k.reshape(tokens_dev, width),
            grad_v.reshape(tokens_dev, width),
        ],
        1,
    ).astype(low_type)
    grad_qbias = jnp.sum(grad_qkv[:, :width].astype(full_type), 0)
    grad_vbias = jnp.sum(grad_qkv[:, 2 * width :].astype(full_type), 0)
    grad_wqkv = contract_rows(start_low, grad_qkv)
    grad_start = grad_middle_in + jnp.dot(grad_qkv, w_qkv.T, preferred_element_type=full_type)
    grad_zhid = grad_zhid + jnp.sum(grad_start * start_norm, 0)
    grad_embed, grad_gain0, grad_shift0 = norm_back(embed, vecs_f[0], vecs_f[1], grad_start * zhid)
    grad_pos = jnp.sum(grad_embed.reshape(row_shape), 0).T
    word_grads = lax.all_gather(grad_embed.astype(low_type), "unit", axis=0, tiled=True)
    local_rows = group_ids - base_row
    inside = (local_rows >= 0) & (local_rows < vocab_slice)
    grad_table = grad_table.at[jnp.where(inside, local_rows, vocab_slice)].add(
        word_grads.astype(full_type), mode="drop"
    )
    grad_hid = gate_back(hid_logit, noise_hid, grad_zhid)
    grad_head = gate_back(masks_r[:heads], noise_head, grad_zhead)
    grad_mha = gate_back(masks_r[heads], gate_noise[width + heads], grad_zmha)
    grad_mlp = gate_back(masks_r[heads + 1], gate_noise[width + heads + 1], grad_zmlp)
    grad_masks = jnp.concatenate([grad_head, grad_mha[None], grad_mlp[None]])
    grad_mats = jnp.concatenate([grad_wqkv, grad_wout, grad_wtrans, grad_pos], 1)
    grad_vecs = jnp.stack(
        [
            grad_gain0,
            grad_shift0,
            grad_qbias,
            grad_vbias,
            grad_obias,
            grad_gain1,
            grad_shift1,
            grad_dbias,
            grad_gain2,
            grad_shift2,
            grad_tbias,
            grad_hgain,
            grad_hshift,
            grad_hid,
        ]
    )
    share_mats, share_vecs = (
        lax.psum_scatter(grad_mats, ("unit", "dp"), scatter_dimension=0, tiled=True),
        lax.psum_scatter(grad_vecs, ("unit", "dp"), scatter_dimension=1, tiled=True),
    )
    share_ffn, share_unit, share_table, share_bias = (
        lax.psum_scatter(
            grad_ffn.astype(jnp.bfloat16), "dp", scatter_dimension=1, tiled=True
        ).astype(jnp.float32),
        lax.psum_scatter(
            grad_unit.astype(jnp.bfloat16), "dp", scatter_dimension=1, tiled=True
        ).astype(jnp.float32),
        lax.psum_scatter(
            grad_table.astype(jnp.bfloat16), "dp", scatter_dimension=1, tiled=True
        ).astype(jnp.float32),
        lax.psum_scatter(
            grad_bias.astype(jnp.bfloat16), "dp", scatter_dimension=0, tiled=True
        ).astype(jnp.float32),
    )
    own_hid = rounded(layer_vecs[13])
    own_unit = rounded(unit_vecs[1])
    lag_hid = (
        lag_slope * (4.0 * head_size * head_sum + 2.0 * unit_sum) / full_size * score_slope(own_hid)
    )
    share_vecs = share_vecs.at[13].add(lag_hid)
    lag_unit = lag_slope * 2.0 * hid_sum * mlp_score / full_size * score_slope(own_unit)
    share_unit = share_unit.at[1].add(lag_unit)
    lag_head = (
        lag_slope * 4.0 * head_size * hid_sum * mha_score / full_size * score_slope(masks_r[:heads])
    )
    lag_mha = (
        lag_slope
        * 4.0
        * head_size
        * hid_sum
        * jnp.sum(head_scores)
        / full_size
        * score_slope(masks_r[heads])
    )
    lag_mlp = lag_slope * 2.0 * hid_sum * stats[5] / full_size * score_slope(masks_r[heads + 1])
    lag_masks = jnp.concatenate([lag_head, lag_mha[None], lag_mlp[None]])
    square_part = sum(
        (
            jnp.sum(item * item)
            for item in (share_mats, share_vecs, share_ffn, share_unit, share_table, share_bias)
        )
    )
    totals = lax.psum((grad_masks, kl_own, square_part), ("unit", "dp"))
    share_masks = totals[0] + lag_masks
    grad_norm = jnp.sqrt(totals[2] + jnp.sum(share_masks * share_masks))
    loss = TEMPER * TEMPER * totals[1] / npos + lagrange
    coef = jnp.minimum(1.0, MAX_NORM / (grad_norm + 1e-06))
    count = step_count[0].astype(full_type)
    mats_grad = share_mats * coef
    vecs_grad = share_vecs * coef
    ffn_grad = share_ffn * coef
    unit_grad = share_unit * coef
    table_grad = share_table * coef
    bias_grad = share_bias * coef
    mask_grad = share_masks * coef
    mats_new = adamw(layer_mats, mats_first, mats_second, mats_grad, RATE_MATS, count)
    vecs_new = adamw(layer_vecs, vecs_first, vecs_second, vecs_grad, RATE_VECS, count)
    ffn_new = adamw(ffn_mats, ffn_first, ffn_second, ffn_grad, RATE_MATS, count)
    unit_new = adamw(unit_vecs, unit_first, unit_second, unit_grad, RATE_VECS, count)
    table_new = adamw(word_table, table_first, table_second, table_grad, RATE_TABLE, count)
    bias_new = adamw(word_bias, bias_first, bias_second, bias_grad, RATE_VECS, count)
    mask_new = adamw(mask_logits, mask_first, mask_second, mask_grad, RATE_VECS, count)
    return (
        loss,
        kept,
        grad_norm,
        mats_new,
        mats_grad,
        vecs_new,
        vecs_grad,
        ffn_new,
        ffn_grad,
        unit_new,
        unit_grad,
        table_new,
        table_grad,
        bias_new,
        bias_grad,
        mask_new,
        mask_grad,
    )


def solution(mesh):
    return jax.shard_map(
        on_device,
        mesh=mesh,
        in_specs=(
            P("dp", None, None),
            P("dp", "unit", None),
            P("dp", "unit", None),
            P("dp", None, None, "unit"),
            P(),
            P(),
            P(),
            P(),
            P(("unit", "dp"), None),
            P(("unit", "dp"), None),
            P(("unit", "dp"), None),
            P(None, ("unit", "dp")),
            P(None, ("unit", "dp")),
            P(None, ("unit", "dp")),
            P(None, "dp", "unit"),
            P(None, "dp", "unit"),
            P(None, "dp", "unit"),
            P(None, ("unit", "dp")),
            P(None, ("unit", "dp")),
            P(None, ("unit", "dp")),
            P("unit", "dp"),
            P("unit", "dp"),
            P("unit", "dp"),
            P(("unit", "dp")),
            P(("unit", "dp")),
            P(("unit", "dp")),
            P(),
            P(),
            P(),
        ),
        out_specs=(
            P(),
            P(),
            P(),
            P(("unit", "dp"), None),
            P(("unit", "dp"), None),
            P(None, ("unit", "dp")),
            P(None, ("unit", "dp")),
            P(None, "dp", "unit"),
            P(None, "dp", "unit"),
            P(None, ("unit", "dp")),
            P(None, ("unit", "dp")),
            P("unit", "dp"),
            P("unit", "dp"),
            P(("unit", "dp")),
            P(("unit", "dp")),
            P(),
            P(),
        ),
        check_vma=False,
    )
```

profile of v0, /device:TPU:0, one launch (start us, length us, event | category | flops | bytes accessed | tf_op | source)
XLA Modules:
  0.0 1482.9 jit_solution(9553546173232351469)
XLA Ops:
  7.3 3.1 convert_element_type.371
  12.0 45.4 %all-gather.17.cloned.1.call-done = bf16[3840,768]{0,1:T(8,128)(2,1)} async-done(((bf16[3840,192]{0,1:T(8,128)(2,1)}), bf16[3840,768]{0,1:T(8,128)(2,1)}) %all-gather.17.cloned.1.call-update) | async-done | bytes 5898256 | tf_op jit(solution)/shard_map/all_gather | solution.py:210
  57.4 8.4 copy.158
  65.9 22.5 %gather_fusion = bf16[4096,768]{1,0:T(8,128)(2,1)} fusion(bf16[3840,768]{1,0:T(8,128)(2,1)} %copy.158, s32[4096]{0:T(1024)S(1)} %broadcast_clamp_fusion), kind=kCustom, calls=%fused_computation | custom fusion | bytes 12599296 | tf_op jit(solution)/shard_map/jit(_take)/gather | solution.py:235
  88.4 8.1 select_convert_fusion
  99.0 42.0 %all-gather.3 = bf16[32,24,14]{1,2,0:T(8,128)(2,1)S(1)} all-gather(bf16[1,24,14]{1,2,0:T(8,128)(2,1)S(1)} %convert_bitcast_fusion.1), channel_id=1, replica_groups=mesh['unit'=8,'dp'=4] {'unit','dp'}, dimensions={0}, use_global_device_ids=true | all-gather | bytes 22176 | tf_op jit(solution)/shard_map/all_gather | solution.py:205
  147.9 105.0 %reduce-scatter.14.cloned.1.call-done = bf16[512,768]{1,0:T(8,128)(2,1)} async-done(((bf16[4096,768]{1,0:T(8,128)(2,1)}), bf16[512,768]{1,0:T(8,128)(2,1)}) %reduce-scatter.14.cloned.1.call-update) | async-done | bytes 786448 | tf_op jit(solution)/shard_map/reduce_scatter | solution.py:236
  256.0 4.3 fusion.32
  264.7 7.6 fusion.189
  272.3 6.1 fusion.55
  279.6 3.7 fusion.184
  284.9 5.2 all-gather.4
  292.2 91.0 %all-gather.21.cloned.1.call-done = bf16[4096,768]{1,0:T(8,128)(2,1)} async-done(((bf16[512,768]{1,0:T(8,128)(2,1)}), bf16[4096,768]{1,0:T(8,128)(2,1)}) %all-gather.21.cloned.1.call-update) | async-done | bytes 6291472 | tf_op jit(solution)/shard_map/all_gather | solution.py:276
  383.2 6.4 convolution_add_fusion
  389.6 2.7 copy-done.123
  392.3 6.5 convolution_convert_fusion.1
  401.5 19.5 %all-reduce.1 = bf16[8]{0:T(256)(128)(2,1)S(1)} all-reduce(bf16[8]{0:T(256)(128)(2,1)S(1)} %dynamic-update-slice.7), channel_id=1, replica_groups=mesh['unit'=8,'dp'=4] {'unit'}, use_global_device_ids=true, to_apply=%add.1 | all-reduce | flops 8 | bytes 32
  422.3 3.0 fusion.34
  427.5 6.1 all-reduce
  435.1 6.7 exponential_reduce_fusion
  442.0 27.0 %all-gather.7 = bf16[8,1,512]{2,1,0:T(2,128)(2,1)S(1)} all-gather(bf16[1,1,512]{2,1,0:T(2,128)(2,1)S(1)} %reshape.676), channel_id=1, replica_groups=mesh['unit'=8,'dp'=4] {'unit'}, dimensions={0}, use_global_device_ids=true | all-gather | bytes 9216 | tf_op jit(solution)/shard_map/all_gather | solution.py:26
  469.6 26.2 %all-gather.8 = bf16[8,1,512]{2,1,0:T(2,128)(2,1)S(1)} all-gather(bf16[1,1,512]{2,1,0:T(2,128)(2,1)S(1)} %reshape.678), channel_id=1, replica_groups=mesh['unit'=8,'dp'=4] {'unit'}, dimensions={0}, use_global_device_ids=true | all-gather | bytes 9216 | tf_op jit(solution)/shard_map/all_gather | solution.py:26
  497.0 18.7 %reduce-scatter.16.cloned.1.call-done = bf16[512,768]{1,0:T(8,128)(2,1)} async-done(((bf16[4096,768]{1,0:T(8,128)(2,1)}), bf16[512,768]{1,0:T(8,128)(2,1)}) %reduce-scatter.16.cloned.1.call-update) | async-done | bytes 786448 | tf_op jit(solution)/shard_map/reduce_scatter | solution.py:286
  524.4 32.4 %all_gather.62 = bf16[512,768]{1,0:T(8,128)(2,1)S(1)} all-gather(bf16[64,768]{1,0:T(8,128)(2,1)S(1)} %add_convert_fusion.1), channel_id=1, replica_groups=mesh['unit'=8,'dp'=4] {'unit'}, dimensions={0}, use_global_device_ids=true | all-gather | bytes 884736 | tf_op jit(solution)/shard_map/all_gather | solution.py:301
  556.8 5.9 fusion.190
  562.8 26.2 %all-gather.5 = bf16[8,1,512]{2,1,0:T(2,128)(2,1)S(1)} all-gather(bf16[1,1,512]{2,1,0:T(2,128)(2,1)S(1)} %reshape.672), channel_id=2, replica_groups=mesh['unit'=8,'dp'=4] {'unit'}, dimensions={0}, use_global_device_ids=true | all-gather | bytes 9216 | tf_op jit(solution)/shard_map/all_gather | solution.py:26
  589.0 3.8 fusion.6
  592.8 26.0 %all-gather.6 = bf16[8,1,512]{2,1,0:T(2,128)(2,1)S(1)} all-gather(bf16[1,1,512]{2,1,0:T(2,128)(2,1)S(1)} %reshape.674), channel_id=3, replica_groups=mesh['unit'=8,'dp'=4] {'unit'}, dimensions={0}, use_global_device_ids=true | all-gather | bytes 9216 | tf_op jit(solution)/shard_map/all_gather | solution.py:26
  618.9 26.0 %all-gather.9 = bf16[8,1,512]{2,1,0:T(2,128)(2,1)S(1)} all-gather(bf16[1,1,512]{2,1,0:T(2,128)(2,1)S(1)} %reshape.680), channel_id=4, replica_groups=mesh['unit'=8,'dp'=4] {'unit'}, dimensions={0}, use_global_device_ids=true | all-gather | bytes 9216 | tf_op jit(solution)/shard_map/all_gather | solution.py:26
  644.9 19.4 %while.8 = (s32[]{:T(128)}, f32[512]{0:T(512)S(1)}, f32[512]{0:T(512)S(1)}, f32[512]{0:T(512)S(1)}, f32[512]{0:T(512)S(1)}, /*index=5*/f32[512]{0:T(512)S(1)}, f...) while((s32[]{:T(128)}, f32[512]{0:T(512)S(1)}, ...), condition=%wide.region_19.20_spmd, body=%wide.region_18.19_spmd.sunk | while | flops 11270 | bytes 56549 | solution.py:34
  664.9 7.6 fusion.173
  674.4 6.8 fusion.52
  681.2 59.7 %reduce-scatter.18.cloned.1.call-done = bf16[64,768]{1,0:T(8,128)(2,1)} async-done(((bf16[512,768]{1,0:T(8,128)(2,1)}), bf16[64,768]{1,0:T(8,128)(2,1)}) %reduce-scatter.18.cloned.1.call-update) | async-done | bytes 98320 | tf_op jit(solution)/shard_map/reduce_scatter | solution.py:329
  755.6 97.7 %all-gather.25.cloned.1.call-done = bf16[4096,768]{1,0:T(8,128)(2,1)} async-done(((bf16[512,768]{1,0:T(8,128)(2,1)}), bf16[4096,768]{1,0:T(8,128)(2,1)}) %all-gather.25.cloned.1.call-update) | async-done | bytes 6291472 | tf_op jit(solution)/shard_map/all_gather | solution.py:359
  853.3 10.9 fusion.175
  865.9 5.4 convolution_convert_fusion
  871.3 116.2 %reduce-scatter.20.cloned.1.call-done = bf16[512,768]{1,0:T(8,128)(2,1)} async-done(((bf16[4096,768]{1,0:T(8,128)(2,1)}), bf16[512,768]{1,0:T(8,128)(2,1)}) %reduce-scatter.20.cloned.1.call-update) | async-done | bytes 786448 | tf_op jit(solution)/shard_map/reduce_scatter | solution.py:368
  987.5 3.5 multiply_reduce_fusion.2
  995.0 6.8 fusion.58
  1001.8 9.2 multiply_reduce_fusion
  1011.0 6.9 multiply_convert_fusion
  1023.6 3.8 multiply_reduce_fusion.4
  1031.1 8.3 fusion.71
  1039.4 5.8 fusion.72
  1046.9 3.1 copy.174
  1050.0 2.7 fusion.84
  1055.3 5.1 pad_maximum_fusion
  1061.5 9.6 fusion.35
  1071.2 57.2 %all-gather.27.cloned.1.call-done = bf16[4096,768]{1,0:T(8,128)(2,1)} async-done(((bf16[512,768]{1,0:T(8,128)(2,1)}), bf16[4096,768]{1,0:T(8,128)(2,1)}) %all-gather.27.cloned.1.call-update) | async-done | bytes 6291472 | tf_op jit(solution)/shard_map/all_gather | solution.py:419
  1128.4 36.8 %scatter_custom_fusion.1 = f32[3840,768]{1,0:T(8,128)} fusion(f32[3840,768]{1,0:T(8,128)} %fusion.35, s32[4096]{0:T(1024)} %bitcast.260, bf16[4096,768]{1,0:T(8,128)(2,1)} %all-gather.27.cloned.1.call-done), kind=kCustom, calls=%fused_computation.16 | custom fusion | flops 6291456 | bytes 18087936 | tf_op jit(solution)/shard_map/scatter-add | solution.py:422
  1165.2 7.7 convert_element_type.446
  1172.9 8.5 copy.191
  1183.7 3.1 copy.178
  1188.4 5.2 copy.176
  1193.8 5.3 copy.175
  1202.3 5.7 all-reduce.3
  1219.4 40.7 %all-reduce.2 = f32[14,768]{1,0:T(8,128)S(1)} all-reduce(f32[14,768]{1,0:T(8,128)S(1)} %stack.59), channel_id=10, replica_groups=mesh['unit'=8,'dp'=4] {'unit','dp'}, use_global_device_ids=true, to_apply=%region_54.55.clone | all-reduce | flops 10752 | bytes 86016
  1261.7 81.2 %reduce-scatter.22.cloned.1.call-done = f32[24,4352]{1,0:T(8,128)} async-done(((f32[768,4352]{1,0:T(8,128)}), f32[24,4352]{1,0:T(8,128)}) %reduce-scatter.22.cloned.1.call-update) | async-done | bytes 417808 | tf_op jit(solution)/shard_map/reduce_scatter | solution.py:450
  1347.2 53.0 %reduce-scatter.28.cloned.1.call-done = bf16[192,3840]{1,0:T(8,128)(2,1)} async-done(((bf16[768,3840]{1,0:T(8,128)(2,1)}), bf16[192,3840]{1,0:T(8,128)(2,1)}) %reduce-scatter.28.cloned.1.call-update) | async-done | bytes 1474576
  1400.1 2.6 copy.192
  1405.6 39.6 %all-reduce.4 = (f32[]{:T(128)}, f32[]{:T(128)}, f32[14]{0:T(128)S(1)}) all-reduce(f32[]{:T(128)} %dynamic-slice_reduce_fusion, f32[]{:T(128)S(6)} %add.708, f32[14]{0:T(128)S(1)} %pad_maximum_fusion.6), channel_id=1, replica_groups=mesh['unit'=8,'dp'=4] {'unit','dp'}, use_global_device_ids=true, to_apply=%region_21.22 | all-reduce | flops 16 | bytes 128 | tf_op jit(solution)/shard_map/psum | solution.py:495
  1447.3 7.8 convert_multiply_fusion.1
  1455.1 5.1 copy.179
  1460.3 5.2 copy.180
  (524 shorter events, 107.0 us)
Async XLA Ops:
  7.2 50.2 %all-gather.17.cloned.1.call-start = ((), (), s32[]{:S(2)}) async-start(), calls=%async_computation.8 | async-start | bytes 7372800 | tf_op jit(solution)/shard_map/all_gather | solution.py:210
  10.4 136.0 %all-gather.19.cloned.1.call-start = ((), (), s32[]{:S(2)}) async-start(), calls=%async_computation.10 | async-start | bytes 6893568 | tf_op jit(solution)/shard_map/all_gather | solution.py:204
  11.2 241.7 %reduce-scatter.14.cloned.1.call-start = ((), (), s32[]{:S(2)}) async-start(), calls=%async_computation.9 | async-start | bytes 7077888 | tf_op jit(solution)/shard_map/reduce_scatter | solution.py:236
  96.5 45.6 %copy-start.61 = (f32[782]{0:T(1024)S(1)}, f32[782]{0:T(1024)}, u32[]{:S(2)}) copy-start(f32[782]{0:T(1024)} %param.39) | copy-start | bytes 9388
  96.5 48.4 %copy-start.83 = (s32[1,1,512]{2,1,0:T(1,128)S(1)}, s32[1,1,512]{2,1,0:T(1,128)}, u32[]{:S(2)}) copy-start(s32[1,1,512]{2,1,0:T(1,128)} %param.36) | copy-start | bytes 6148
  96.5 195.7 %all-gather.23.cloned.1.call-start = ((), (), s32[]{:S(2)}) async-start(), calls=%async_computation.12 | async-start | bytes 1474560 | tf_op jit(solution)/shard_map/all_gather | solution.py:208
  98.3 284.9 %all-gather.21.cloned.1.call-start = ((), (), s32[]{:S(2)}) async-start(), calls=%async_computation.11 | async-start | bytes 7077888 | tf_op jit(solution)/shard_map/all_gather | solution.py:276
  142.1 112.3 %copy-start.54 = (f32[768]{0:T(1024)}, f32[768]{0:T(1024)S(1)}, u32[]{:S(2)}) copy-start(f32[768]{0:T(1024)S(1)} %get-tuple-element.543) | copy-start | bytes 9220
  142.1 137.5 %copy-start.71 = (f32[768]{0:T(1024)}, f32[768]{0:T(1024)S(1)}, u32[]{:S(2)}) copy-start(f32[768]{0:T(1024)S(1)} %get-tuple-element.545) | copy-start | bytes 9220
  142.1 137.5 %copy-start.92 = (f32[768]{0:T(1024)}, f32[768]{0:T(1024)S(1)}, u32[]{:S(2)}) copy-start(f32[768]{0:T(1024)S(1)} %get-tuple-element.544) | copy-start | bytes 9220
  142.1 373.6 %copy-start.52 = (f32[768]{0:T(1024)}, f32[768]{0:T(1024)S(1)}, u32[]{:S(2)}) copy-start(f32[768]{0:T(1024)S(1)} %get-tuple-element.537) | copy-start | bytes 9220
  142.1 375.8 %copy-start.46 = (f32[768]{0:T(1024)}, f32[768]{0:T(1024)S(1)}, u32[]{:S(2)}) copy-start(f32[768]{0:T(1024)S(1)} %get-tuple-element.532) | copy-start | bytes 9220
  146.4 133.1 %copy-start.73 = (f32[768]{0:T(1024)}, f32[768]{0:T(1024)S(1)}, u32[]{:S(2)}) copy-start(f32[768]{0:T(1024)S(1)} %mul.1104) | copy-start | bytes 9220
  147.9 131.7 %copy-start.4 = (bf16[768,512]{0,1:T(8,128)(2,1)}, bf16[768,512]{0,1:T(8,128)(2,1)S(1)}, u32[]{:S(2)}) copy-start(bf16[768,512]{0,1:T(8,128)(2,1)S(1)} %copy.198) | copy-start | bytes 2359300
  254.4 25.2 %copy-start.63 = (f32[512]{0:T(512)}, f32[512]{0:T(512)S(1)}, u32[]{:S(2)}) copy-start(f32[512]{0:T(512)S(1)} %broadcast_multiply_fusion.4) | copy-start | bytes 6148
  255.9 23.6 %copy-start.85 = (f32[512]{0:T(512)}, f32[512]{0:T(512)S(1)}, u32[]{:S(2)}) copy-start(f32[512]{0:T(512)S(1)} %fusion.140) | copy-start | bytes 6148
  283.3 232.4 %copy-start.41 = (f32[512]{0:T(512)}, f32[512]{0:T(512)S(1)}, u32[]{:S(2)}) copy-start(f32[512]{0:T(512)S(1)} %broadcast_multiply_fusion.3) | copy-start | bytes 6148
  283.6 106.0 %copy-start.67 = (f32[512]{0:T(512)}, f32[512]{0:T(512)S(1)}, u32[]{:S(2)}) copy-start(f32[512]{0:T(512)S(1)} %multiply_reduce_fusion.14) | copy-start | bytes 6148
  283.6 232.1 %copy-start.48 = (f32[512]{0:T(512)}, f32[512]{0:T(512)S(1)}, u32[]{:S(2)}) copy-start(f32[512]{0:T(512)S(1)} %fusion.141) | copy-start | bytes 6148
  284.8 230.8 %reduce-scatter.16.cloned.1.call-start = ((), (), s32[]{:S(2)}) async-start(), calls=%async_computation.13 | async-start | bytes 7077888 | tf_op jit(solution)/shard_map/reduce_scatter | solution.py:286
  292.2 97.4 %copy-start.99 = (f32[384]{0:T(512)}, f32[384]{0:T(512)S(1)}, u32[]{:S(2)}) copy-start(f32[384]{0:T(512)S(1)} %get-tuple-element.621) | copy-start | bytes 4612
  398.8 27.1 %copy-start.79 = (f32[960]{0:T(1024)S(1)}, f32[960]{0:T(1024)}, u32[]{:S(2)}) copy-start(f32[960]{0:T(1024)} %param.58) | copy-start | bytes 11524
  398.9 27.1 %copy-start.97 = (u32[32]{0:T(128)S(1)}, u32[32]{0:T(128)}, u32[]{:S(2)}) copy-start(u32[32]{0:T(128)} %constant.418) | copy-start | bytes 388
  398.9 342.0 %reduce-scatter.18.cloned.1.call-start = ((), (), s32[]{:S(2)}) async-start(), calls=%async_computation.14 | async-start | bytes 884736 | tf_op jit(solution)/shard_map/reduce_scatter | solution.py:329
  421.0 21.0 %copy-start.118 = (bf16[8]{0:T(256)(128)(2,1)}, bf16[8]{0:T(256)(128)(2,1)S(1)}, u32[]{:S(2)}) copy-start(bf16[8]{0:T(256)(128)(2,1)S(1)} %all-reduce.1) | copy-start | bytes 52
  435.1 61.2 %copy-start.116 = (s32[1,1,64]{2,1,0:T(1,128)S(1)}, s32[1,1,64]{2,1,0:T(1,128)}, u32[]{:S(2)}) copy-start(s32[1,1,64]{2,1,0:T(1,128)} %param.37) | copy-start | bytes 772
  496.4 19.3 %copy-start.111 = (s32[64]{0:T(128)}, s32[64]{0:T(128)S(1)}, u32[]{:S(2)}) copy-start(s32[64]{0:T(128)S(1)} %fusion.158) | copy-start | bytes 772
  521.1 35.7 %copy-start.78 = (f32[3840]{0:T(1024)S(1)}, f32[3840]{0:T(1024)}, u32[]{:S(2)}) copy-start(f32[3840]{0:T(1024)} %convert_element_type.400) | copy-start | bytes 46084
  524.4 64.6 %slice-start = ((s8[7864320]{0:T(1024)(128)(4,1)}), s8[4194304]{0:T(1024)(128)(4,1)S(1)}, s32[]{:S(2)}) async-start(s8[7864320]{0:T(1024)(128)(4,1)} %bitcast.214), calls=%async_computation.22 | async-start | bytes 8388608
  556.8 32.2 %slice-start.1 = ((s8[7864320]{0:T(1024)(128)(4,1)}), s8[3670016]{0:T(1024)(128)(4,1)S(1)}, s32[]{:S(2)}) async-start(s8[7864320]{0:T(1024)(128)(4,1)} %bitcast.214), calls=%async_computation.23 | async-start | bytes 7340032
  556.8 32.3 %copy-start.84 = (f32[512]{0:T(512)S(1)}, f32[512]{0:T(512)}, u32[]{:S(2)}) copy-start(f32[512]{0:T(512)} %sub.385) | copy-start | bytes 6148
  562.7 30.1 %copy-start = (f32[512,3840]{1,0:T(8,128)}, f32[512,3840]{1,0:T(8,128)S(1)}, u32[]{:S(2)}) copy-start(f32[512,3840]{1,0:T(8,128)S(1)} %get-tuple-element.659) | copy-start | bytes 23592964
  589.0 55.9 %copy-start.40 = (f32[1,1,512]{2,1,0:T(1,128)S(1)}, f32[1,1,512]{2,1,0:T(1,128)}, u32[]{:S(2)}) copy-start(f32[1,1,512]{2,1,0:T(1,128)} %slice_convert_fusion.2) | copy-start | bytes 6148
  589.0 55.9 %copy-start.119 = (bf16[8]{0:T(256)(128)(2,1)S(1)}, bf16[8]{0:T(256)(128)(2,1)}, u32[]{:S(2)}) copy-start(bf16[8]{0:T(256)(128)(2,1)} %copy-done.118) | copy-start | bytes 52
  674.3 66.6 %copy-start.82 = (f32[64]{0:T(128)S(1)}, f32[64]{0:T(128)}, u32[]{:S(2)}) copy-start(f32[64]{0:T(128)} %copy-done.81) | copy-start | bytes 772
  674.3 68.2 %copy-start.106 = (f32[64]{0:T(128)S(1)}, f32[64]{0:T(128)}, u32[]{:S(2)}) copy-start(f32[64]{0:T(128)} %copy-done.105) | copy-start | bytes 772
  674.3 68.2 %copy-start.91 = (f32[64]{0:T(128)S(1)}, f32[64]{0:T(128)}, u32[]{:S(2)}) copy-start(f32[64]{0:T(128)} %copy-done.90) | copy-start | bytes 772
  681.2 68.8 %copy-start.47 = (f32[768]{0:T(1024)S(1)}, f32[768]{0:T(1024)}, u32[]{:S(2)}) copy-start(f32[768]{0:T(1024)} %copy-done.46) | copy-start | bytes 9220
  681.2 172.1 %all-gather.25.cloned.1.call-start = ((), (), s32[]{:S(2)}) async-start(), calls=%async_computation.15 | async-start | bytes 7077888 | tf_op jit(solution)/shard_map/all_gather | solution.py:359
  752.8 100.5 %copy-start.100 = (f32[384]{0:T(512)S(1)}, f32[384]{0:T(512)}, u32[]{:S(2)}) copy-start(f32[384]{0:T(512)} %copy-done.99) | copy-start | bytes 4612
  752.8 100.5 %copy-start.115 = (bf16[2,768,384]{2,1,0:T(8,128)(2,1)S(1)}, bf16[2,768,384]{2,1,0:T(8,128)(2,1)}, u32[]{:S(2)}) copy-start(bf16[2,768,384]{2,1,0:T(8,128)(2,1)} %all-gather.23.cloned.1.call-done) | copy-start | bytes 3538948
  755.1 232.4 %reduce-scatter.20.cloned.1.call-start = ((), (), s32[]{:S(2)}) async-start(), calls=%async_computation.16 | async-start | bytes 7077888 | tf_op jit(solution)/shard_map/reduce_scatter | solution.py:368
  871.2 116.3 %copy-start.2 = (f32[512,768]{1,0:T(8,128)S(1)}, f32[512,768]{1,0:T(8,128)}, u32[]{:S(2)}) copy-start(f32[512,768]{1,0:T(8,128)} %copy-done.1) | copy-start | bytes 4718596
  871.2 116.3 %copy-start.42 = (f32[512]{0:T(512)S(1)}, f32[512]{0:T(512)}, u32[]{:S(2)}) copy-start(f32[512]{0:T(512)} %copy-done.41) | copy-start | bytes 6148
  871.2 116.3 %copy-start.49 = (f32[512]{0:T(512)S(1)}, f32[512]{0:T(512)}, u32[]{:S(2)}) copy-start(f32[512]{0:T(512)} %copy-done.48) | copy-start | bytes 6148
  871.2 116.3 %copy-start.53 = (f32[768]{0:T(1024)S(1)}, f32[768]{0:T(1024)}, u32[]{:S(2)}) copy-start(f32[768]{0:T(1024)} %copy-done.52) | copy-start | bytes 9220
  871.3 119.8 %copy-start.68 = (f32[512]{0:T(512)S(1)}, f32[512]{0:T(512)}, u32[]{:S(2)}) copy-start(f32[512]{0:T(512)} %copy-done.67) | copy-start | bytes 6148
  871.3 257.1 %all-gather.27.cloned.1.call-start = ((), (), s32[]{:S(2)}) async-start(), calls=%async_computation.19 | async-start | bytes 7077888 | tf_op jit(solution)/shard_map/all_gather | solution.py:419
  995.0 16.0 %slice-start.2 = ((s8[12582912]{0:T(1024)(128)(4,1)}), s8[4194304]{0:T(1024)(128)(4,1)S(1)}, s32[]{:S(2)}) async-start(s8[12582912]{0:T(1024)(128)(4,1)} %bitcast.217), calls=%async_computation.24 | async-start | bytes 8388608
  995.0 16.0 %slice-start.3 = ((s8[12582912]{0:T(1024)(128)(4,1)}), s8[4194304]{0:T(1024)(128)(4,1)S(1)}, s32[]{:S(2)}) async-start(s8[12582912]{0:T(1024)(128)(4,1)} %bitcast.217), calls=%async_computation.25 | async-start | bytes 8388608
  1001.8 19.4 %copy-start.32 = (bf16[12,64,512]{2,1,0:T(8,128)(2,1)}, bf16[12,64,512]{2,1,0:T(8,128)(2,1)S(1)}, u32[]{:S(2)}) copy-start(bf16[12,64,512]{2,1,0:T(8,128)(2,1)S(1)} %fusion.58) | copy-start | bytes 2359300
  1030.0 178.8 %reduce-scatter.26.cloned.1.call-start = ((), (), s32[]{:S(2)}) async-start(), calls=%async_computation.20 | async-start | bytes 122880
  1031.0 178.6 %reduce-scatter.24.cloned.1.call-start = ((), (), s32[]{:S(2)}) async-start(), calls=%async_computation.18 | async-start | bytes 1474560 | tf_op jit(solution)/shard_map/reduce_scatter | solution.py:454
  1046.4 296.4 %reduce-scatter.22.cloned.1.call-start = ((), (), s32[]{:S(2)}) async-start(), calls=%async_computation.17 | async-start | bytes 13787136 | tf_op jit(solution)/shard_map/reduce_scatter | solution.py:450
  1060.4 339.7 %reduce-scatter.28.cloned.1.call-start = ((), (), s32[]{:S(2)}) async-start(), calls=%async_computation.21 | async-start | bytes 7372800
  1193.7 15.0 %copy-start.77 = (f32[768]{0:T(1024)S(1)}, f32[768]{0:T(1024)}, u32[]{:S(2)}) copy-start(f32[768]{0:T(1024)} %get-tuple-element.604) | copy-start | bytes 9220
  1193.7 15.1 %copy-start.76 = (f32[768]{0:T(1024)S(1)}, f32[768]{0:T(1024)}, u32[]{:S(2)}) copy-start(f32[768]{0:T(1024)} %get-tuple-element.528) | copy-start | bytes 9220
  1193.7 15.1 %copy-start.75 = (f32[768]{0:T(1024)S(1)}, f32[768]{0:T(1024)}, u32[]{:S(2)}) copy-start(f32[768]{0:T(1024)} %get-tuple-element.530) | copy-start | bytes 9220
  1193.7 17.7 %copy-start.55 = (f32[768]{0:T(1024)S(1)}, f32[768]{0:T(1024)}, u32[]{:S(2)}) copy-start(f32[768]{0:T(1024)} %copy-done.54) | copy-start | bytes 9220
  1193.7 17.7 %copy-start.62 = (f32[782]{0:T(1024)S(1)}, f32[782]{0:T(1024)}, u32[]{:S(2)}) copy-start(f32[782]{0:T(1024)} %param.39) | copy-start | bytes 9388
  1193.7 22.9 %copy-start.14 = (bf16[12,64,512]{2,1,0:T(8,128)(2,1)S(1)}, bf16[12,64,512]{2,1,0:T(8,128)(2,1)}, u32[]{:S(2)}) copy-start(bf16[12,64,512]{2,1,0:T(8,128)(2,1)} %copy-done.12) | copy-start | bytes 2359300
  1193.7 23.1 %copy-start.34 = (bf16[12,64,512]{2,1,0:T(8,128)(2,1)S(1)}, bf16[12,64,512]{2,1,0:T(8,128)(2,1)}, u32[]{:S(2)}) copy-start(bf16[12,64,512]{2,1,0:T(8,128)(2,1)} %copy-done.32) | copy-start | bytes 2359300
  1199.0 61.3 %copy-start.113 = (f32[12]{0:T(128)S(1)}, f32[12]{0:T(128)}, u32[]{:S(2)}) copy-start(f32[12]{0:T(128)} %get-tuple-element.648) | copy-start | bytes 148
  1199.0 62.6 %copy-start.112 = (f32[12]{0:T(128)S(1)}, f32[12]{0:T(128)}, u32[]{:S(2)}) copy-start(f32[12]{0:T(128)} %get-tuple-element.603) | copy-start | bytes 148
  (81 other events, 338.9 us)
Sparse Core Ops, SparseCore 0:
  10.5 46.8 all-gather.16
  60.9 71.7 all-gather.18
  136.3 116.5 reduce-scatter.13
  254.9 16.5 all-gather.22
  284.9 98.1 all-gather.20
  399.0 116.6 reduce-scatter.15
  681.3 59.5 reduce-scatter.17
  755.2 98.0 all-gather.24
  871.4 116.0 reduce-scatter.19
  1030.2 98.1 all-gather.26
  1131.5 17.6 reduce-scatter.25
  1151.8 25.7 reduce-scatter.23
  1183.7 159.1 reduce-scatter.21
  1345.4 54.6 reduce-scatter.27
where the time goes:
time: 1490 us; the launch traced here: 1480 us
  waiting for transfers between devices  725 us (49%)
  blocking collectives  323 us (22%)
  other arithmetic  159 us (11%)
  matrix products  122 us (8%)
  local copies, waits for them, and re-layouts  106 us (7%)
  between operations  41.7 us (3%)
    all_gather x5, blocking collectives, joined(): lax.all_gather(part.astype(kind), axis)  131 us
    reduce_scatter x1, waiting for transfers between devices, on_device(): lax.psum_scatter(jnp.dot(grad_hpre_low, up_w.T, preferred_element_type=fu...  116 us
    reduce_scatter x1, waiting for transfers between devices, on_device(): lax.psum_scatter(jnp.where(inside[:, None], found.astype(full_type), 0.0)...  105 us
    all_gather x1, waiting for transfers between devices, on_device(): back_all = lax.all_gather(grad_fout, 'unit', axis=0, tiled=True)  97.7 us
    all_gather x1, waiting for transfers between devices, on_device(): rows_all = lax.all_gather(middle_low, 'unit', axis=0, tiled=True)  91 us
    reduce_scatter x1, waiting for transfers between devices, on_device(): lax.psum_scatter(grad_mats, ('unit', 'dp'), scatter_dimension=0, tiled=True)  81.2 us
    unnamed x4, blocking collectives  72.2 us
    reduce_scatter x1, waiting for transfers between devices, on_device(): lax.psum_scatter(jnp.dot(grad_logit_low, table_group, preferred_element_t...  59.7 us
  transfers between devices with their start and end apart: 14, of which 10 were waited for; matrix products, arithmetic and copies ran while one was open for 14% of the time, Pallas kernels for 0%

commit v1 on v0

v1 whole, which is shorter than its diff:
```python
import functools
import math

import jax
import jax.numpy as jnp
from jax import lax
from jax.experimental import pallas as pl
from jax.experimental.pallas import tpu as pltpu
from jax.sharding import PartitionSpec as P

EPS_NORM = 1e-12
GAMMA = -0.1
ZETA = 1.1
BETA = 2.0 / 3.0
TARGET = 0.95
TEMPER = 2.0
MAX_NORM = 0.0001
BETA_ONE = 0.9
BETA_TWO = 0.999
ADAM_EPS = 1e-08
DECAY = 0.01
RATE_MATS = 0.5
RATE_VECS = 5.0
RATE_TABLE = 1.0


MESH = pl.DeviceIdType.MESH
VMEM_LIMIT = 56 * 1024 * 1024


def on_chip():
    return pl.BlockSpec(memory_space=pltpu.VMEM)


def call_params(collective):
    return pltpu.CompilerParams(
        collective_id=collective, has_side_effects=True, vmem_limit_bytes=VMEM_LIMIT
    )


def greet_unit(n, me):
    barrier = pltpu.get_barrier_semaphore()

    def step(j, carry):
        pl.semaphore_signal(
            barrier, inc=1, device_id={"unit": lax.rem(me + j, n)}, device_id_type=MESH
        )
        return carry

    lax.fori_loop(1, n, step, 0)
    pl.semaphore_wait(barrier, n - 1)


def greet_all(nu, nd, me):
    barrier = pltpu.get_barrier_semaphore()

    def step(j, carry):
        peer = lax.rem(me + j, nu * nd)
        pl.semaphore_signal(
            barrier,
            inc=1,
            device_id={"unit": peer // nd, "dp": lax.rem(peer, nd)},
            device_id_type=MESH,
        )
        return carry

    lax.fori_loop(1, nu * nd, step, 0)
    pl.semaphore_wait(barrier, nu * nd - 1)


def gather_kernel(n, x_ref, out_ref, send_sem, recv_sem):
    me = lax.axis_index("unit")
    greet_unit(n, me)

    def copy(peer, slot):
        return pltpu.make_async_remote_copy(
            src_ref=x_ref,
            dst_ref=out_ref.at[slot],
            send_sem=send_sem.at[peer],
            recv_sem=recv_sem.at[slot],
            device_id={"unit": peer},
            device_id_type=MESH,
        )

    def start(j, carry):
        copy(lax.rem(me + j, n), me).start()
        return carry

    def wait(j, carry):
        peer = lax.rem(me + j, n)
        copy(peer, me).wait_send()
        copy(peer, peer).wait_recv()
        return carry

    lax.fori_loop(1, n, start, 0)
    out_ref[me] = x_ref[...]
    lax.fori_loop(1, n, wait, 0)


def gather_unit(x, n, collective):
    return pl.pallas_call(
        functools.partial(gather_kernel, n),
        out_shape=jax.ShapeDtypeStruct((n,) + x.shape, x.dtype),
        in_specs=[on_chip()],
        out_specs=on_chip(),
        scratch_shapes=[pltpu.SemaphoreType.DMA((n,)), pltpu.SemaphoreType.DMA((n,))],
        compiler_params=call_params(collective),
    )(x)


def scatter_kernel(n, x_ref, out_ref, held, send_sem, recv_sem):
    me = lax.axis_index("unit")
    greet_unit(n, me)

    def copy(peer, slot):
        return pltpu.make_async_remote_copy(
            src_ref=x_ref.at[peer],
            dst_ref=held.at[slot],
            send_sem=send_sem.at[peer],
            recv_sem=recv_sem.at[slot],
            device_id={"unit": peer},
            device_id_type=MESH,
        )

    def start(j, carry):
        copy(lax.rem(me + j, n), me).start()
        return carry

    def wait(j, carry):
        peer = lax.rem(me + j, n)
        copy(peer, me).wait_send()
        copy(peer, peer).wait_recv()
        return carry

    lax.fori_loop(1, n, start, 0)
    held[me] = x_ref[me]
    lax.fori_loop(1, n, wait, 0)
    out_ref[...] = jnp.zeros_like(out_ref)

    def add(j, carry):
        out_ref[...] += held[j].astype(jnp.float32)
        return carry

    lax.fori_loop(0, n, add, 0)


def scatter_unit(x, n, collective):
    return pl.pallas_call(
        functools.partial(scatter_kernel, n),
        out_shape=jax.ShapeDtypeStruct(x.shape[1:], jnp.float32),
        in_specs=[on_chip()],
        out_specs=on_chip(),
        scratch_shapes=[
            pltpu.VMEM(x.shape, x.dtype),
            pltpu.SemaphoreType.DMA((n,)),
            pltpu.SemaphoreType.DMA((n,)),
        ],
        compiler_params=call_params(collective),
    )(x)


def total_kernel(nu, nd, x_ref, out_ref, held, send_sem, recv_sem):
    n = nu * nd
    me = lax.axis_index("unit") * nd + lax.axis_index("dp")
    greet_all(nu, nd, me)

    def copy(peer, slot):
        return pltpu.make_async_remote_copy(
            src_ref=x_ref,
            dst_ref=held.at[slot],
            send_sem=send_sem.at[peer],
            recv_sem=recv_sem.at[slot],
            device_id={"unit": peer // nd, "dp": lax.rem(peer, nd)},
            device_id_type=MESH,
        )

    def start(j, carry):
        copy(lax.rem(me + j, n), me).start()
        return carry

    def wait(j, carry):
        peer = lax.rem(me + j, n)
        copy(peer, me).wait_send()
        copy(peer, peer).wait_recv()
        return carry

    lax.fori_loop(1, n, start, 0)
    held[me] = x_ref[...]
    lax.fori_loop(1, n, wait, 0)
    out_ref[...] = jnp.zeros_like(out_ref)

    def add(j, carry):
        out_ref[...] += held[j]
        return carry

    lax.fori_loop(0, n, add, 0)


def total_all(x, nu, nd, collective):
    n = nu * nd
    return pl.pallas_call(
        functools.partial(total_kernel, nu, nd),
        out_shape=jax.ShapeDtypeStruct(x.shape, x.dtype),
        in_specs=[on_chip()],
        out_specs=on_chip(),
        scratch_shapes=[
            pltpu.VMEM((n,) + x.shape, x.dtype),
            pltpu.SemaphoreType.DMA((n,)),
            pltpu.SemaphoreType.DMA((n,)),
        ],
        compiler_params=call_params(collective),
    )(x)


def fetch_kernel(
    nu, nd, cap, wanted, table, out, asked, match, rows, send_a, recv_a, send_b, recv_b, own_sem
):
    n = nu * nd
    my_unit = lax.axis_index("unit")
    my_dp = lax.axis_index("dp")
    me = my_unit * nd + my_dp
    vocab = table.shape[0]
    block = 1280 if vocab % 1280 == 0 else vocab
    greet_all(nu, nd, me)

    def ask(peer, slot):
        return pltpu.make_async_remote_copy(
            src_ref=wanted.at[peer // nd],
            dst_ref=asked.at[slot],
            send_sem=send_a.at[peer],
            recv_sem=recv_a.at[slot],
            device_id={"unit": peer // nd, "dp": lax.rem(peer, nd)},
            device_id_type=MESH,
        )

    def answer(unit, dp, from_unit, from_dp):
        peer = unit * nd + dp
        return pltpu.make_async_remote_copy(
            src_ref=rows.at[peer],
            dst_ref=out.at[from_dp, from_unit],
            send_sem=send_b.at[peer],
            recv_sem=recv_b.at[from_unit * nd + from_dp],
            device_id={"unit": unit, "dp": dp},
            device_id_type=MESH,
        )

    def ask_start(j, carry):
        ask(lax.rem(me + j, n), me).start()
        return carry

    def ask_wait(j, carry):
        peer = lax.rem(me + j, n)
        ask(peer, me).wait_send()
        ask(peer, peer).wait_recv()
        return carry

    lax.fori_loop(1, n, ask_start, 0)
    asked[me] = wanted[my_unit]
    lax.fori_loop(1, n, ask_wait, 0)

    def one_group(g, carry):
        dp = lax.rem(my_dp + g, nd)
        total = jnp.zeros((nu * cap, table.shape[1]), jnp.float32)
        for start in range(0, vocab, block):
            lanes = lax.broadcasted_iota(jnp.int32, (cap, block), 1) + start
            for unit in range(nu):
                ids = jnp.swapaxes(
                    jnp.broadcast_to(asked[unit * nd + dp], (8, 128)), 0, 1
                )[:cap, :1]
                match[unit * cap : (unit + 1) * cap, :] = jnp.where(
                    ids == lanes, 1.0, 0.0
                ).astype(jnp.bfloat16)
            total = total + jnp.dot(
                match[...], table[start : start + block, :], preferred_element_type=jnp.float32
            )
        for unit in range(nu):
            rows[unit * nd + dp] = total[unit * cap : (unit + 1) * cap].astype(jnp.bfloat16)

        def send(unit, carry):
            @pl.when(jnp.logical_or(unit != my_unit, dp != my_dp))
            def _():
                answer(unit, dp, my_unit, my_dp).start()

            return carry

        lax.fori_loop(0, nu, send, 0)
        return carry

    lax.fori_loop(0, nd, one_group, 0)
    own = pltpu.make_async_copy(rows.at[me], out.at[my_dp, my_unit], own_sem)
    own.start()
    own.wait()

    def answer_wait(j, carry):
        peer = lax.rem(me + j, n)
        unit, dp = peer // nd, lax.rem(peer, nd)
        answer(unit, dp, my_unit, my_dp).wait_send()
        answer(unit, dp, unit, dp).wait_recv()
        return carry

    lax.fori_loop(1, n, answer_wait, 0)


def fetch_rows(wanted, table, nu, nd, cap, collective):
    n = nu * nd
    vocab, part = table.shape
    block = 1280 if vocab % 1280 == 0 else vocab
    return pl.pallas_call(
        functools.partial(fetch_kernel, nu, nd, cap),
        out_shape=(
            jax.ShapeDtypeStruct((nd, nu, cap, part), jnp.bfloat16),
            jax.ShapeDtypeStruct((n, 1, 128), jnp.int32),
        ),
        in_specs=[on_chip(), on_chip()],
        out_specs=(on_chip(), on_chip()),
        scratch_shapes=[
            pltpu.VMEM((nu * cap, block), jnp.bfloat16),
            pltpu.VMEM((n, cap, part), jnp.bfloat16),
            pltpu.SemaphoreType.DMA((n,)),
            pltpu.SemaphoreType.DMA((n,)),
            pltpu.SemaphoreType.DMA((n,)),
            pltpu.SemaphoreType.DMA((n,)),
            pltpu.SemaphoreType.DMA,
        ],
        compiler_params=call_params(collective),
    )(wanted, table)


def return_kernel(nu, nd, x_ref, out_ref, send_sem, recv_sem, own_sem):
    n = nu * nd
    my_unit = lax.axis_index("unit")
    my_dp = lax.axis_index("dp")
    me = my_unit * nd + my_dp
    greet_all(nu, nd, me)

    def copy(peer, slot):
        unit, dp = peer // nd, lax.rem(peer, nd)
        return pltpu.make_async_remote_copy(
            src_ref=x_ref.at[dp, unit],
            dst_ref=out_ref.at[slot],
            send_sem=send_sem.at[peer],
            recv_sem=recv_sem.at[slot],
            device_id={"unit": unit, "dp": dp},
            device_id_type=MESH,
        )

    def start(j, carry):
        copy(lax.rem(me + j, n), me).start()
        return carry

    def wait(j, carry):
        peer = lax.rem(me + j, n)
        copy(peer, me).wait_send()
        copy(peer, peer).wait_recv()
        return carry

    lax.fori_loop(1, n, start, 0)
    own = pltpu.make_async_copy(x_ref.at[my_dp, my_unit], out_ref.at[me], own_sem)
    own.start()
    own.wait()
    lax.fori_loop(1, n, wait, 0)


def return_rows(x, nu, nd, collective):
    n = nu * nd
    return pl.pallas_call(
        functools.partial(return_kernel, nu, nd),
        out_shape=jax.ShapeDtypeStruct((n,) + x.shape[2:], x.dtype),
        in_specs=[on_chip()],
        out_specs=on_chip(),
        scratch_shapes=[
            pltpu.SemaphoreType.DMA((n,)),
            pltpu.SemaphoreType.DMA((n,)),
            pltpu.SemaphoreType.DMA,
        ],
        compiler_params=call_params(collective),
    )(x)


def rounded(values):
    return lax.optimization_barrier(values.astype(jnp.bfloat16)).astype(jnp.float32)


def layer_norm(values, gain, shift):
    center = values - jnp.mean(values, -1, keepdims=True)
    spread = jnp.mean(center * center, -1, keepdims=True)
    return center * lax.rsqrt(spread + EPS_NORM) * gain + shift


def norm_back(values, gain, shift, grad):
    _, pull = jax.vjp(layer_norm, values, gain, shift)
    return pull(grad)


def gelu_back(values, grad):
    _, pull = jax.vjp(jax.nn.gelu, values)
    return pull(grad)[0]


def gate(logit, noise):
    soft = jax.nn.sigmoid((jnp.log(noise) - jnp.log(1.0 - noise) + logit) / BETA)
    return jnp.clip(soft * (ZETA - GAMMA) + GAMMA, 0.0, 1.0)


def gate_back(logit, noise, grad):
    _, pull = jax.vjp(gate, logit, noise)
    return pull(grad)[0]


def keep_score(logit):
    return jax.nn.sigmoid(logit - BETA * math.log(-GAMMA / ZETA))


def score_slope(logit):
    score = keep_score(logit)
    return score * (1.0 - score)


def contract_rows(left, right):
    return lax.dot_general(
        left, right, (((0,), (0,)), ((), ())), preferred_element_type=jnp.float32
    )


def adamw(weight, first, second, grad, rate, count):
    first = BETA_ONE * first + (1.0 - BETA_ONE) * grad
    second = BETA_TWO * second + (1.0 - BETA_TWO) * grad * grad
    first_hat = first / (1.0 - BETA_ONE**count)
    second_hat = second / (1.0 - BETA_TWO**count)
    return weight - rate * (first_hat / (jnp.sqrt(second_hat) + ADAM_EPS) + DECAY * weight)


def on_device(
    token_ids,
    segments,
    positions,
    teacher,
    gate_noise,
    unit_noise,
    multipliers,
    step_count,
    layer_mats,
    mats_first,
    mats_second,
    layer_vecs,
    vecs_first,
    vecs_second,
    ffn_mats,
    ffn_first,
    ffn_second,
    unit_vecs,
    unit_first,
    unit_second,
    word_table,
    table_first,
    table_second,
    word_bias,
    bias_first,
    bias_second,
    mask_logits,
    mask_first,
    mask_second,
):
    low_type = jnp.bfloat16
    full_type = jnp.float32
    exact = lax.Precision.HIGHEST
    units_n = lax.axis_size("unit")
    groups_n = lax.axis_size("dp")
    everyone = ("unit", "dp")
    heads = mask_logits.shape[0] - 2
    share_rows = layer_mats.shape[0]
    width = share_rows * units_n * groups_n
    head_size = width // heads
    seq_len = segments.shape[2]
    nmask = positions.shape[2]
    unit_idx = lax.axis_index("unit")
    n_vecs = layer_vecs.shape[0]
    vec_pad = -n_vecs % 128
    vocab_slice = word_table.shape[0]
    table_part = word_table.shape[1]
    cap = 16 * -(-5 * seq_len // (4 * 16 * units_n))

    mats_low = layer_mats.astype(low_type)
    qkv_cols = 3 * width
    trans_end = 5 * width
    table_low = word_table.astype(low_type)
    first_send = jnp.concatenate(
        [
            mats_low[:, :qkv_cols],
            mats_low[:, trans_end:],
            jnp.pad(layer_vecs.T, ((0, 0), (0, vec_pad))).astype(low_type),
        ],
        1,
    )
    first_all = lax.all_gather(first_send, everyone, axis=0, tiled=True)
    second_all = lax.all_gather(mats_low[:, qkv_cols:trans_end], everyone, axis=0, tiled=True)
    small_len = unit_vecs.size + word_bias.size
    ffn_cols = ffn_mats.shape[2]
    small_rows = -(-small_len // (16 * ffn_cols)) * 16
    ffn_rows = ffn_mats.shape[1]
    slice_pack = jnp.concatenate(
        [
            ffn_mats.reshape(2 * ffn_rows, ffn_cols),
            jnp.pad(
                jnp.concatenate([unit_vecs.reshape(-1), word_bias]),
                (0, small_rows * ffn_cols - small_len),
            ).reshape(small_rows, ffn_cols),
        ],
        0,
    ).astype(low_type)
    slice_all = lax.all_gather(slice_pack, "dp", axis=0)
    table_cols = lax.all_gather(table_low.T, "dp", axis=0, tiled=True)

    ids = lax.dynamic_index_in_dim(token_ids[0], unit_idx, 0, keepdims=False)
    place = jnp.arange(seq_len, dtype=jnp.int32)
    same_id = ids[:, None] == ids[None, :]
    first_place = jnp.min(jnp.where(same_id, place[None, :], seq_len), 1)
    is_first = first_place == place
    owner = ids // vocab_slice
    slot = jnp.sum(
        (
            is_first[None, :]
            & (owner[None, :] == owner[:, None])
            & (place[None, :] < first_place[:, None])
        ).astype(jnp.int32),
        1,
    )
    slots_used = jnp.max(slot) + 1
    local_id = ids - owner * vocab_slice
    entry = jnp.arange(units_n * cap, dtype=jnp.int32)

    def round_match(k):
        here = slot - k * cap
        code = jnp.where((here >= 0) & (here < cap), owner * cap + here, -1)
        return entry[:, None] == code[None, :]

    def round_wanted(match):
        return jnp.max(
            jnp.where(match & is_first[None, :], local_id[None, :], -1), 1
        ).reshape(units_n, cap)

    match_0 = round_match(0)
    wanted_0 = jnp.concatenate(
        [
            round_wanted(match_0),
            jnp.broadcast_to(slots_used, (units_n, 128 - cap)),
        ],
        1,
    )[:, None, :]
    fetched, asked = fetch_rows(wanted_0, table_low, units_n, groups_n, cap, 1)
    asked = asked[:, 0, :]
    rounds = (jnp.max(asked[:, cap:]) + cap - 1) // cap
    match_0 = match_0.astype(low_type)

    def spread(match, parts):
        return jnp.concatenate(
            [
                contract_rows(match, parts[d].reshape(units_n * cap, table_part))
                for d in range(groups_n)
            ],
            1,
        )

    def round_asked(match):
        wanted_all = lax.all_gather(round_wanted(match), everyone, axis=0)
        return lax.dynamic_index_in_dim(wanted_all, unit_idx, 1, keepdims=False)

    def more_words(k, words):
        match = round_match(k)
        mine = round_asked(match)
        found = jnp.where(
            (mine >= 0)[:, :, None], jnp.take(table_low, jnp.maximum(mine, 0), axis=0), 0
        )
        found = lax.all_to_all(found, everyone, 0, 0, tiled=True)
        found = jnp.swapaxes(
            found.reshape(units_n, groups_n, cap, table_part), 0, 1
        )
        return words + spread(match.astype(low_type), found)

    word = lax.fori_loop(1, rounds, more_words, spread(match_0, fetched))

    vecs_f = first_all[:, qkv_cols + seq_len : qkv_cols + seq_len + n_vecs].T.astype(full_type)
    masks_r = rounded(mask_logits)
    hid_logit = vecs_f[13]
    noise_hid = gate_noise[:width]
    noise_head = gate_noise[width : width + heads]
    zhid = gate(hid_logit, noise_hid)
    zhead = gate(masks_r[:heads], noise_head)
    zmha = gate(masks_r[heads], gate_noise[width + heads])
    zmlp = gate(masks_r[heads + 1], gate_noise[width + heads + 1])
    w_q = first_all[:, :width]
    w_kv = first_all[:, width:qkv_cols]
    w_out = second_all[:, :width]
    w_trans = second_all[:, width:]
    pos_table = first_all[:, qkv_cols : qkv_cols + seq_len].T.astype(full_type)
    embed = word + pos_table
    start_norm = layer_norm(embed, vecs_f[0], vecs_f[1])
    start = start_norm * zhid
    start_low = start.astype(low_type)

    picks = positions.reshape(-1)
    pick_low = (picks[:, None] == place[None, :]).astype(low_type)
    pick_full = pick_low.astype(full_type)
    start_p = jnp.dot(pick_full, start, precision=exact, preferred_element_type=full_type)
    start_p_low = start_p.astype(low_type)
    seg = segments.reshape(-1)
    seg_p = jnp.sum(jnp.where(picks[:, None] == place[None, :], seg[None, :], 0), 1)
    same = seg_p[:, None] == seg[None, :]
    queries = (
        jnp.dot(start_p_low, w_q, preferred_element_type=full_type) + vecs_f[2]
    ).astype(low_type)
    kv = jnp.dot(start_low, w_kv, preferred_element_type=full_type)
    keys_b = kv[:, :width].astype(low_type)
    values_b = (kv[:, width:] + vecs_f[3]).astype(low_type)
    scale = head_size ** (-0.5)
    q3 = queries.reshape(nmask, heads, head_size)
    k3 = keys_b.reshape(seq_len, heads, head_size)
    v3 = values_b.reshape(seq_len, heads, head_size)
    scores = jnp.einsum("qhd,khd->hqk", q3, k3, preferred_element_type=full_type) * scale
    probs = jax.nn.softmax(jnp.where(same[None], scores, -1000000000.0), axis=-1)
    probs_low = probs.astype(low_type)
    context = jnp.einsum(
        "hqk,khd->qhd", probs_low, v3, preferred_element_type=full_type
    ).reshape(nmask, width)
    context_r = context
    zcols = jnp.repeat(zhead, head_size)
    scaled = (context_r * zcols).astype(low_type)
    attn_res = jnp.dot(scaled, w_out, preferred_element_type=full_type) + vecs_f[4]
    middle_in = start_p + attn_res * zmha * zhid
    middle = layer_norm(middle_in, vecs_f[5], vecs_f[6])
    rows_all = gather_unit(middle.astype(low_type), units_n, 2).reshape(-1, width)

    up_w = slice_all[:, :ffn_rows].reshape(width, ffn_cols)
    down_w = slice_all[:, ffn_rows : 2 * ffn_rows].reshape(width, ffn_cols)
    small = slice_all[:, 2 * ffn_rows :].reshape(groups_n, -1)
    unit_group = jnp.swapaxes(
        small[:, : unit_vecs.size].reshape(groups_n, 2, unit_vecs.shape[1]), 0, 1
    ).reshape(2, -1)
    bias_group = small[:, unit_vecs.size : small_len].reshape(-1).astype(full_type)
    unit_bias = unit_group[0].astype(full_type)
    unit_logit = unit_group[1].astype(full_type)
    slice_units = unit_bias.shape[0]
    ffn_width = slice_units * units_n
    noise_units = lax.dynamic_slice_in_dim(unit_noise, unit_idx * slice_units, slice_units, 0)
    zunit = gate(unit_logit, noise_units)
    hidden_pre = jnp.dot(rows_all, up_w, preferred_element_type=full_type) + unit_bias
    hidden_gelu = jax.nn.gelu(hidden_pre)
    hidden = (hidden_gelu * zunit).astype(low_type)
    rows3 = (units_n, nmask, width)
    ffn_out = scatter_unit(
        jnp.dot(hidden, down_w.T, preferred_element_type=full_type)
        .astype(low_type)
        .reshape(rows3),
        units_n,
        3,
    )
    ffn_res = ffn_out + vecs_f[7]
    final_in = middle + ffn_res * zmlp * zhid
    final = layer_norm(final_in, vecs_f[8], vecs_f[9])
    picked = final.astype(low_type)
    trans_pre = jnp.dot(picked, w_trans, preferred_element_type=full_type) + vecs_f[10]
    trans_gelu = jax.nn.gelu(trans_pre)
    trans_low = layer_norm(trans_gelu, vecs_f[11], vecs_f[12]).astype(low_type)
    trans_all = gather_unit(trans_low, units_n, 4).reshape(-1, width)

    student = (
        jnp.dot(trans_all, table_cols, preferred_element_type=full_type) + bias_group
    ) / TEMPER
    teach = teacher.reshape(-1, vocab_slice).astype(full_type) / TEMPER
    s_max = jnp.max(student, -1)
    s_sum = jnp.sum(jnp.exp(student - s_max[:, None]), -1)
    t_max = jnp.max(teach, -1)
    t_exp = jnp.exp(teach - t_max[:, None])
    t_sum = jnp.sum(t_exp, -1)
    cross = jnp.sum(t_exp * (teach - student), -1)
    unit_part = jnp.sum(keep_score(unit_logit))
    stats = gather_unit(
        jnp.concatenate(
            [
                jnp.stack([s_max, s_sum, t_max, t_sum, cross]),
                jnp.broadcast_to(unit_part, (3, s_max.shape[0])),
            ],
            0,
        ),
        units_n,
        5,
    )
    s_top = jnp.max(stats[:, 0], 0)
    t_top = jnp.max(stats[:, 2], 0)
    s_all = jnp.sum(stats[:, 1] * jnp.exp(stats[:, 0] - s_top), 0)
    t_scale = jnp.exp(stats[:, 2] - t_top)
    t_all = jnp.sum(stats[:, 3] * t_scale, 0)
    cross_all = jnp.sum(stats[:, 4] * t_scale, 0)
    unit_score = jnp.sum(stats[:, 5, 0])
    lse_student = s_top + jnp.log(s_all)
    lse_teach = t_top + jnp.log(t_all)
    kl_rows = cross_all / t_all - lse_teach + lse_student
    kl_own = jnp.sum(lax.dynamic_slice_in_dim(kl_rows, unit_idx * nmask, nmask, 0))
    npos = groups_n * kl_rows.shape[0]
    grad_logit = (
        TEMPER
        / npos
        * (jnp.exp(student - lse_student[:, None]) - jnp.exp(teach - lse_teach[:, None]))
    )
    grad_bias = jnp.sum(grad_logit, 0)
    grad_logit_low = grad_logit.astype(low_type)
    grad_trans = scatter_unit(
        lax.dot_general(
            grad_logit_low,
            table_cols,
            (((1,), (1,)), ((), ())),
            preferred_element_type=full_type,
        )
        .astype(low_type)
        .reshape(rows3),
        units_n,
        6,
    )
    grad_table = contract_rows(trans_all, grad_logit_low).astype(low_type)
    share_head = lax.psum_scatter(grad_table, "dp", scatter_dimension=0, tiled=True)

    hid_sum = jnp.sum(keep_score(hid_logit))
    head_scores = keep_score(masks_r[:heads])
    mha_score = keep_score(masks_r[heads])
    mlp_score = keep_score(masks_r[heads + 1])
    head_sum = jnp.sum(head_scores) * mha_score
    unit_sum = unit_score * mlp_score
    full_size = 4.0 * width * width + 2.0 * width * ffn_width
    kept = (4.0 * head_size * hid_sum * head_sum + 2.0 * hid_sum * unit_sum) / full_size
    sparsity = 1.0 - kept
    lagrange = multipliers[0] * (sparsity - TARGET) + multipliers[1] * (sparsity - TARGET) ** 2
    lag_slope = -(multipliers[0] + 2.0 * multipliers[1] * (sparsity - TARGET))
    grad_tgelu, grad_hgain, grad_hshift = norm_back(trans_gelu, vecs_f[11], vecs_f[12], grad_trans)
    grad_tpre = gelu_back(trans_pre, grad_tgelu)
    grad_tbias = jnp.sum(grad_tpre, 0)
    grad_tpre_low = grad_tpre.astype(low_type)
    grad_wtrans = contract_rows(picked, grad_tpre_low)
    grad_final = jnp.dot(grad_tpre_low, w_trans.T, preferred_element_type=full_type)
    grad_final_in, grad_gain2, grad_shift2 = norm_back(final_in, vecs_f[8], vecs_f[9], grad_final)
    grad_fres = grad_final_in * zmlp * zhid
    grad_dbias = jnp.sum(grad_fres, 0)
    grad_zmlp = jnp.sum(grad_final_in * ffn_res * zhid)
    grad_zhid = jnp.sum(grad_final_in * ffn_res * zmlp, 0)
    back_all = gather_unit(grad_fres.astype(low_type), units_n, 7).reshape(-1, width)
    grad_hidden = jnp.dot(back_all, down_w, preferred_element_type=full_type)
    grad_hpre = gelu_back(hidden_pre, grad_hidden * zunit)
    grad_hpre_low = grad_hpre.astype(low_type)
    grad_middle_ffn = scatter_unit(
        jnp.dot(grad_hpre_low, up_w.T, preferred_element_type=full_type)
        .astype(low_type)
        .reshape(rows3),
        units_n,
        8,
    )
    grad_down = contract_rows(back_all, hidden)
    grad_up = contract_rows(rows_all, grad_hpre_low)
    grad_zunit = jnp.sum(grad_hidden * hidden_gelu, 0)
    grad_ubias = jnp.sum(grad_hpre, 0)
    grad_ulogit = gate_back(unit_logit, noise_units, grad_zunit)
    small_grads = jnp.concatenate(
        [
            jnp.swapaxes(
                jnp.stack([grad_ubias, grad_ulogit]).reshape(2, groups_n, -1), 0, 1
            ).reshape(groups_n, -1),
            grad_bias.reshape(groups_n, -1),
        ],
        1,
    )
    slice_grads = jnp.concatenate(
        [
            grad_up.astype(low_type).reshape(groups_n, ffn_rows, ffn_cols),
            grad_down.astype(low_type).reshape(groups_n, ffn_rows, ffn_cols),
            jnp.pad(small_grads, ((0, 0), (0, small_rows * ffn_cols - small_len)))
            .astype(low_type)
            .reshape(groups_n, small_rows, ffn_cols),
        ],
        1,
    )
    share_slice = lax.psum_scatter(slice_grads, "dp", scatter_dimension=0, tiled=False).astype(
        full_type
    )

    grad_middle_in, grad_gain1, grad_shift1 = norm_back(
        middle_in, vecs_f[5], vecs_f[6], grad_final_in + grad_middle_ffn
    )
    grad_ares = grad_middle_in * zmha * zhid
    grad_obias = jnp.sum(grad_ares, 0)
    grad_zmha = jnp.sum(grad_middle_in * attn_res * zhid)
    grad_zhid = grad_zhid + jnp.sum(grad_middle_in * attn_res * zmha, 0)
    grad_ares_low = grad_ares.astype(low_type)
    grad_wout = contract_rows(scaled, grad_ares_low)
    share_second = lax.psum_scatter(
        jnp.concatenate([grad_wout, grad_wtrans], 1).astype(low_type),
        everyone,
        scatter_dimension=0,
        tiled=True,
    ).astype(full_type)
    grad_scaled = jnp.dot(grad_ares_low, w_out.T, preferred_element_type=full_type)
    grad_zhead = jnp.sum((grad_scaled * context_r).reshape(nmask, heads, head_size), axis=(0, 2))
    g3 = (grad_scaled * zcols).astype(low_type).reshape(nmask, heads, head_size)
    grad_probs = jnp.einsum("qhd,khd->hqk", g3, v3, preferred_element_type=full_type)
    grad_scores = (probs * (grad_probs - jnp.sum(grad_probs * probs, -1, keepdims=True))).astype(
        low_type
    )
    grad_q = (
        jnp.einsum("hqk,khd->qhd", grad_scores, k3, preferred_element_type=full_type) * scale
    ).reshape(nmask, width)
    grad_k = (
        jnp.einsum("hqk,qhd->khd", grad_scores, q3, preferred_element_type=full_type) * scale
    ).reshape(seq_len, width)
    grad_v = jnp.einsum("hqk,qhd->khd", probs_low, g3, preferred_element_type=full_type).reshape(
        seq_len, width
    )
    grad_q_low = grad_q.astype(low_type)
    grad_kv = jnp.concatenate([grad_k, grad_v], 1).astype(low_type)
    grad_qbias = jnp.sum(grad_q_low.astype(full_type), 0)
    grad_vbias = jnp.sum(grad_kv[:, width:].astype(full_type), 0)
    grad_wq = contract_rows(start_p_low, grad_q_low)
    grad_wkv = contract_rows(start_low, grad_kv)
    grad_start_p = grad_middle_in + jnp.dot(grad_q_low, w_q.T, preferred_element_type=full_type)
    grad_start = lax.dot_general(
        pick_full,
        grad_start_p,
        (((0,), (0,)), ((), ())),
        precision=exact,
        preferred_element_type=full_type,
    ) + jnp.dot(grad_kv, w_kv.T, preferred_element_type=full_type)
    grad_zhid = grad_zhid + jnp.sum(grad_start * start_norm, 0)
    grad_embed, grad_gain0, grad_shift0 = norm_back(embed, vecs_f[0], vecs_f[1], grad_start * zhid)
    grad_hid = gate_back(hid_logit, noise_hid, grad_zhid)
    grad_vecs = jnp.stack(
        [
            grad_gain0,
            grad_shift0,
            grad_qbias,
            grad_vbias,
            grad_obias,
            grad_gain1,
            grad_shift1,
            grad_dbias,
            grad_gain2,
            grad_shift2,
            grad_tbias,
            grad_hgain,
            grad_hshift,
            grad_hid,
        ]
    )
    share_first = lax.psum_scatter(
        jnp.concatenate(
            [
                grad_wq.astype(low_type),
                grad_wkv.astype(low_type),
                grad_embed.T.astype(low_type),
                jnp.pad(grad_vecs.T, ((0, 0), (0, vec_pad))).astype(low_type),
            ],
            1,
        ),
        everyone,
        scatter_dimension=0,
        tiled=True,
    ).astype(full_type)

    embed_low = grad_embed.astype(low_type)

    def word_parts(match):
        return jnp.stack(
            [
                jnp.dot(
                    match,
                    embed_low[:, d * table_part : (d + 1) * table_part],
                    preferred_element_type=full_type,
                )
                .astype(low_type)
                .reshape(units_n, cap, table_part)
                for d in range(groups_n)
            ]
        )

    returned = return_rows(word_parts(match_0), units_n, groups_n, 9).reshape(-1, table_part)
    asked_ids = asked[:, :cap].reshape(-1)
    hit = (jnp.arange(vocab_slice, dtype=jnp.int32)[:, None] == asked_ids[None, :]).astype(low_type)
    share_table = share_head.astype(full_type).T + jnp.dot(
        hit, returned, preferred_element_type=full_type
    )

    def more_grads(k, total):
        match = round_match(k)
        mine = round_asked(match).reshape(-1)
        back = jnp.swapaxes(word_parts(match.astype(low_type)), 0, 1).reshape(
            units_n * groups_n, cap, table_part
        )
        back = lax.all_to_all(back, everyone, 0, 0, tiled=True).reshape(-1, table_part)
        target = jnp.where(mine >= 0, mine, vocab_slice)
        return total.at[target].add(back.astype(full_type), mode="drop")

    share_table = lax.fori_loop(1, rounds, more_grads, share_table)

    grad_head = gate_back(masks_r[:heads], noise_head, grad_zhead)
    grad_mha = gate_back(masks_r[heads], gate_noise[width + heads], grad_zmha)
    grad_mlp = gate_back(masks_r[heads + 1], gate_noise[width + heads + 1], grad_zmlp)
    share_mats = jnp.concatenate(
        [share_first[:, :qkv_cols], share_second, share_first[:, qkv_cols : qkv_cols + seq_len]], 1
    )
    share_vecs = share_first[:, qkv_cols + seq_len : qkv_cols + seq_len + n_vecs].T
    share_ffn = share_slice[: 2 * ffn_rows].reshape(2, ffn_rows, ffn_cols)
    share_small = share_slice[2 * ffn_rows :].reshape(-1)
    share_unit = share_small[: unit_vecs.size].reshape(unit_vecs.shape)
    share_bias = share_small[unit_vecs.size : small_len]
    own_hid = rounded(layer_vecs[13])
    own_unit = rounded(unit_vecs[1])
    lag_hid = (
        lag_slope * (4.0 * head_size * head_sum + 2.0 * unit_sum) / full_size * score_slope(own_hid)
    )
    share_vecs = share_vecs.at[13].add(lag_hid)
    lag_unit = lag_slope * 2.0 * hid_sum * mlp_score / full_size * score_slope(own_unit)
    share_unit = share_unit.at[1].add(lag_unit)
    lag_head = (
        lag_slope * 4.0 * head_size * hid_sum * mha_score / full_size * score_slope(masks_r[:heads])
    )
    lag_mha = (
        lag_slope
        * 4.0
        * head_size
        * hid_sum
        * jnp.sum(head_scores)
        / full_size
        * score_slope(masks_r[heads])
    )
    lag_mlp = lag_slope * 2.0 * hid_sum * unit_score / full_size * score_slope(masks_r[heads + 1])
    lag_masks = jnp.concatenate([lag_head, lag_mha[None], lag_mlp[None]])
    square_part = sum(
        (
            jnp.sum(item * item)
            for item in (share_mats, share_vecs, share_ffn, share_unit, share_table, share_bias)
        )
    )
    mine = jnp.concatenate(
        [grad_head, grad_mha[None], grad_mlp[None], kl_own[None], square_part[None]]
    )
    n_masks = heads + 2
    totals = total_all(
        jnp.pad(mine, (0, 1024 - mine.shape[0])).reshape(8, 128), units_n, groups_n, 10
    )[0]
    share_masks = totals[:n_masks] + lag_masks
    grad_norm = jnp.sqrt(totals[n_masks + 1] + jnp.sum(share_masks * share_masks))
    loss = TEMPER * TEMPER * totals[n_masks] / npos + lagrange
    coef = jnp.minimum(1.0, MAX_NORM / (grad_norm + 1e-06))
    count = step_count[0].astype(full_type)
    mats_grad = share_mats * coef
    vecs_grad = share_vecs * coef
    ffn_grad = share_ffn * coef
    unit_grad = share_unit * coef
    table_grad = share_table * coef
    bias_grad = share_bias * coef
    mask_grad = share_masks * coef
    mats_new = adamw(layer_mats, mats_first, mats_second, mats_grad, RATE_MATS, count)
    vecs_new = adamw(layer_vecs, vecs_first, vecs_second, vecs_grad, RATE_VECS, count)
    ffn_new = adamw(ffn_mats, ffn_first, ffn_second, ffn_grad, RATE_MATS, count)
    unit_new = adamw(unit_vecs, unit_first, unit_second, unit_grad, RATE_VECS, count)
    table_new = adamw(word_table, table_first, table_second, table_grad, RATE_TABLE, count)
    bias_new = adamw(word_bias, bias_first, bias_second, bias_grad, RATE_VECS, count)
    mask_new = adamw(mask_logits, mask_first, mask_second, mask_grad, RATE_VECS, count)
    return (
        loss,
        kept,
        grad_norm,
        mats_new,
        mats_grad,
        vecs_new,
        vecs_grad,
        ffn_new,
        ffn_grad,
        unit_new,
        unit_grad,
        table_new,
        table_grad,
        bias_new,
        bias_grad,
        mask_new,
        mask_grad,
    )


def solution(mesh):
    return jax.shard_map(
        on_device,
        mesh=mesh,
        in_specs=(
            P("dp", None, None),
            P("dp", "unit", None),
            P("dp", "unit", None),
            P("dp", None, None, "unit"),
            P(),
            P(),
            P(),
            P(),
            P(("unit", "dp"), None),
            P(("unit", "dp"), None),
            P(("unit", "dp"), None),
            P(None, ("unit", "dp")),
            P(None, ("unit", "dp")),
            P(None, ("unit", "dp")),
            P(None, "dp", "unit"),
            P(None, "dp", "unit"),
            P(None, "dp", "unit"),
            P(None, ("unit", "dp")),
            P(None, ("unit", "dp")),
            P(None, ("unit", "dp")),
            P("unit", "dp"),
            P("unit", "dp"),
            P("unit", "dp"),
            P(("unit", "dp")),
            P(("unit", "dp")),
            P(("unit", "dp")),
            P(),
            P(),
            P(),
        ),
        out_specs=(
            P(),
            P(),
            P(),
            P(("unit", "dp"), None),
            P(("unit", "dp"), None),
            P(None, ("unit", "dp")),
            P(None, ("unit", "dp")),
            P(None, "dp", "unit"),
            P(None, "dp", "unit"),
            P(None, ("unit", "dp")),
            P(None, ("unit", "dp")),
            P("unit", "dp"),
            P("unit", "dp"),
            P(("unit", "dp")),
            P(("unit", "dp")),
            P(),
            P(),
        ),
        check_vma=False,
    )
```

time: 1490 us -> 733 us (0.49)
  waiting for transfers between devices: 725 us -> 220 us
  blocking collectives: 323 us -> 0 us
  Pallas kernels: 0 us -> 231 us
  other arithmetic: 159 us -> 93.7 us
  local copies, waits for them, and re-layouts: 106 us -> 58.2 us
  matrix products: 122 us -> 79.4 us
    reduce_scatter x6 -> x2, waiting for transfers between devices: 381 us -> 49.5 us  [the longest x1 49.5 us: on_device(): lax.psum_scatter(grad_table, 'dp', scatter_dimension=0, tiled=True)]
    all_gather x6 -> x4, waiting for transfers between devices: 291 us -> 32.7 us  [the longest x1 32.7 us: on_device(): lax.all_gather(mats_low[:, qkv_cols:trans_end], everyone, axis=0, tiled=T...]
    pallas_call x0 -> x10, Pallas kernels: none -> 231 us  [the longest x4 73.9 us: gather_unit(): pl.pallas_call(functools.partial(gather_kernel, n), out_shape=jax.ShapeDt...]
    all_gather x8 -> x0, blocking collectives: 211 us -> none  [the longest x5 131 us: joined(): lax.all_gather(part.astype(kind), axis)]
    unnamed x16 -> x10, waiting for transfers between devices: 53.2 us -> 137 us
    unnamed x4 -> x0, blocking collectives: 72.2 us -> none
    psum x1 -> x0, blocking collectives: 39.6 us -> none  [on_device(): totals = lax.psum((grad_masks, kl_own, square_part), ('unit', 'dp'))]
    scatter-add x2 -> x0, other arithmetic: 39.1 us -> none  [the longest x1 36.8 us: on_device(): grad_table.at[jnp.where(inside, local_rows, vocab_slice)]]
  transfers between devices with their start and end apart: 14 -> 8, of which waited for: 10 -> 4; matrix products, arithmetic and copies ran while one was open for 14% -> 18% of each run, Pallas kernels for 0% -> 24%
where the time goes in v1:
time: 733 us; the launch traced here: 726 us
  Pallas kernels  231 us (32%)
  waiting for transfers between devices  220 us (30%)
  other arithmetic  93.7 us (13%)
  matrix products  79.4 us (11%)
  local copies, waits for them, and re-layouts  58.2 us (8%)
  between operations  43.1 us (6%)
    unnamed x10, waiting for transfers between devices  137 us
    pallas_call x4, Pallas kernels, gather_unit(): pl.pallas_call(functools.partial(gather_kernel, n), out_shape=jax.ShapeDt...  73.9 us
    pallas_call x3, Pallas kernels, scatter_unit(): pl.pallas_call(functools.partial(scatter_kernel, n), out_shape=jax.ShapeD...  60.4 us
    pallas_call x1, Pallas kernels, fetch_rows(): pl.pallas_call(functools.partial(fetch_kernel, nu, nd, cap), out_shape=(j...  51.1 us
    reduce_scatter x1, waiting for transfers between devices, on_device(): lax.psum_scatter(grad_table, 'dp', scatter_dimension=0, tiled=True)  49.5 us
    pallas_call x1, Pallas kernels, return_rows(): pl.pallas_call(functools.partial(return_kernel, nu, nd), out_shape=jax.Sh...  35.3 us
    all_gather x1, waiting for transfers between devices, on_device(): lax.all_gather(mats_low[:, qkv_cols:trans_end], everyone, axis=0, tiled=T...  32.7 us
    unnamed x301, local copies, waits for them, and re-layouts  20.6 us
  transfers between devices with their start and end apart: 8, of which 4 were waited for; matrix products, arithmetic and copies ran while one was open for 18% of the time, Pallas kernels for 24%

profile of v1, /device:TPU:0, one launch (start us, length us, event | category | flops | bytes accessed | tf_op | source)
XLA Modules:
  0.0 726.0 jit_solution(1935267120460469303)
XLA Ops:
  13.0 2.9 copy.394.table
  15.9 2.1 copy.400
  22.3 3.0 fusion.45
  29.4 51.1 %shard_map.404 = (bf16[4,8,80,192]{3,2,1,0:T(8,128)(2,1)}, s32[32,1,128]{2,1,0:T(1,128)}) custom-call(s32[8,1,128]{2,1,0:T(1,128)} %bitcast.324, bf16[3840,192]{1,0:T(8,128)(2,1)S(1)} %copy.394.table), custom_call_target="tpu_custom_call" | custom-call | tf_op jit(solution)/shard_map/pallas_call | solution.py:308
  80.5 1.4 slice_reduce_fusion.14
  82.7 7.2 exponential_reduce_fusion
  96.8 2.3 pad_maximum_fusion.1
  103.5 2.4 fusion.237
  106.1 1.9 fusion.234
  109.3 3.3 slice_reduce_fusion.1
  114.0 1.6 fusion.81
  115.8 3.3 fusion.54
  119.1 1.7 copy-done.13
  122.1 1.5 fusion.60
  124.7 3.0 fusion.243
  127.8 1.8 fusion.123
  129.8 32.7 %all-gather.7.cloned.1.call-done = bf16[768,1536]{1,0:T(8,128)(2,1)} async-done(((bf16[24,1536]{1,0:T(8,128)(2,1)}), bf16[768,1536]{1,0:T(8,128)(2,1)}) %all-gather.7.cloned.1.call-update) | async-done | bytes 2359312 | tf_op jit(solution)/shard_map/all_gather | solution.py:496
  162.5 1.8 fusion.233
  165.8 18.4 %shard_map.405 = bf16[8,64,768]{2,1,0:T(8,128)(2,1)} custom-call(bf16[64,768]{1,0:T(8,128)(2,1)} %fusion.143.x_ref), custom_call_target="tpu_custom_call" | custom-call | tf_op jit(solution)/shard_map/pallas_call | solution.py:101
  184.2 1.7 convolution_add_fusion.1
  186.0 1.6 convolution_convert_fusion.7
  187.6 22.8 %shard_map.406 = f32[64,768]{1,0:T(8,128)} custom-call(bf16[8,64,768]{2,1,0:T(8,128)(2,1)} %bitcast.300), custom_call_target="tpu_custom_call" | custom-call | tf_op jit(solution)/shard_map/pallas_call | solution.py:148
  214.0 22.2 %shard_map.407 = bf16[8,64,768]{2,1,0:T(8,128)(2,1)} custom-call(bf16[64,768]{1,0:T(8,128)(2,1)} %add_convert_fusion.1.x_ref), custom_call_target="tpu_custom_call" | custom-call | tf_op jit(solution)/shard_map/pallas_call | solution.py:101
  236.2 6.0 fusion.244
  242.3 4.3 fusion.39
  249.3 12.3 %shard_map.408 = f32[8,8,512]{2,1,0:T(8,128)} custom-call(f32[8,512]{1,0:T(8,128)} %concatenate.77.x_ref), custom_call_target="tpu_custom_call" | custom-call | tf_op jit(solution)/shard_map/pallas_call | solution.py:101
  263.5 7.6 %fusion.223 = (bf16[3840]{0:T(1024)(128)(2,1)}, bf16[512,3840]{1,0:T(8,128)(2,1)S(1)}) fusion(f32[512]{0:T(512)S(1)} %get-tuple-element.709, f32[1,8,64,3840]{3,2,1,0:T(8,128)} %get-tuple-element.689, f32[512,3840]{1,0:T(8,128)} %copy-done.4, f32[512]{0:T(512)S(1)} %get-tuple-element.662), kind=kLoop, calls=%fused_computation.441 | loop fusion | flops 11792640 | bytes 19672576 | tf_op jit(solution)/shard_map/reduce_sum | solution.py:705
  271.0 8.2 %fusion.64 = bf16[512,768]{1,0:T(8,128)(2,1)} fusion(bf16[768,3840]{1,0:T(8,128)(2,1)} %all-gather.11.cloned.1.call-done, bf16[512,3840]{1,0:T(8,128)(2,1)S(1)} %get-tuple-element.654), kind=kOutput, calls=%fused_computation.118 | convolution fusion | flops 3020292096 | bytes 10616832 | tf_op jit(solution)/shard_map/dot_general | solution.py:708
  279.3 16.2 %shard_map.409 = f32[64,768]{1,0:T(8,128)} custom-call(bf16[8,64,768]{2,1,0:T(8,128)(2,1)} %bitcast.299), custom_call_target="tpu_custom_call" | custom-call | tf_op jit(solution)/shard_map/pallas_call | solution.py:148
  295.5 1.7 multiply_reduce_fusion.12
  300.5 1.4 multiply_reduce_fusion.11
  301.9 21.0 %shard_map.410 = bf16[8,64,768]{2,1,0:T(8,128)(2,1)} custom-call(bf16[64,768]{1,0:T(8,128)(2,1)} %get-tuple-element.697.x_ref), custom_call_target="tpu_custom_call" | custom-call | tf_op jit(solution)/shard_map/pallas_call | solution.py:101
  323.0 2.9 fusion.221
  325.9 1.5 convolution_convert_fusion.8
  327.4 1.4 convolution_convert_fusion.9
  328.8 1.5 convolution_convert_fusion.6
  332.8 2.4 pad_maximum_fusion.4
  335.3 21.4 %shard_map.411 = f32[64,768]{1,0:T(8,128)} custom-call(bf16[8,64,768]{2,1,0:T(8,128)(2,1)} %bitcast.274), custom_call_target="tpu_custom_call" | custom-call | tf_op jit(solution)/shard_map/pallas_call | solution.py:148
  356.8 1.7 multiply_reduce_fusion.14
  361.3 1.6 pad_maximum_fusion
  362.8 4.4 copy.427
  367.2 2.0 multiply_reduce_fusion.4
  373.2 4.4 fusion.52
  379.1 1.9 convolution_add_fusion.2
  381.0 3.0 multiply_reduce_fusion.3
  385.5 1.6 copy.412
  387.1 1.9 fusion.226
  390.4 1.5 convolution_convert_fusion.1
  392.0 2.4 fusion.44
  395.5 7.3 %convolution_convert_fusion = bf16[768,3840]{1,0:T(8,128)(2,1)} fusion(bf16[512,768]{1,0:T(8,128)(2,1)S(1)} %bitcast.290, bf16[512,3840]{1,0:T(8,128)(2,1)} %copy-done.8), kind=kOutput, calls=%fused_computation.69 | convolution fusion | flops 3022848000 | bytes 10616832 | tf_op jit(solution)/shard_map/dot_general | solution.py:420
  421.9 35.3 %shard_map.412 = bf16[32,80,192]{2,1,0:T(8,128)(2,1)} custom-call(bf16[4,8,80,192]{3,2,1,0:T(8,128)(2,1)} %pad_maximum_fusion.3.x_ref), custom_call_target="tpu_custom_call" | custom-call | tf_op jit(solution)/shard_map/pallas_call | solution.py:366
  462.7 32.4 %reduce-scatter.13.cloned.1.call-done = bf16[24,1536]{1,0:T(8,128)(2,1)} async-done(((bf16[768,1536]{1,0:T(8,128)(2,1)}), bf16[24,1536]{1,0:T(8,128)(2,1)}) %reduce-scatter.13.cloned.1.call-update) | async-done | bytes 73744
  497.1 104.9 %reduce-scatter.15.cloned.1.call-done = bf16[24,2944]{1,0:T(8,128)(2,1)} async-done(((bf16[768,2944]{1,0:T(8,128)(2,1)}), bf16[24,2944]{1,0:T(8,128)(2,1)}) %reduce-scatter.15.cloned.1.call-update) | async-done | bytes 141328
  609.9 49.5 %reduce-scatter.11.cloned.1.call-done = bf16[192,3840]{1,0:T(8,128)(2,1)} async-done(((bf16[768,3840]{1,0:T(8,128)(2,1)}), bf16[192,3840]{1,0:T(8,128)(2,1)}) %reduce-scatter.11.cloned.1.call-update) | async-done | bytes 1474576 | tf_op jit(solution)/shard_map/reduce_scatter | solution.py:720
  659.4 10.7 %fusion.43 = f32[3840,192]{0,1:T(8,128)S(1)} fusion(bf16[2560,192]{1,0:T(8,128)(2,1)} %bitcast.283, s32[2560]{0:T(1024)S(1)} %eq.221, bf16[192,3840]{1,0:T(8,128)(2,1)} %reduce-scatter.11.cloned.1.call-done), kind=kOutput, calls=%fused_computation.70 | convolution fusion | flops 3786178560 | bytes 5416960 | tf_op jit(solution)/shard_map/dot_general | solution.py:883
  670.1 3.1 copy.422
  673.5 3.7 multiply_reduce_fusion
  677.3 3.4 copy.424
  683.3 10.4 %shard_map.413 = f32[8,128]{1,0:T(8,128)} custom-call(f32[8,128]{1,0:T(8,128)} %pad_bitcast_fusion.x_ref), custom_call_target="tpu_custom_call" | custom-call | tf_op jit(solution)/shard_map/pallas_call | solution.py:201
  695.1 1.9 multiply_reduce_fusion.27
  698.3 1.9 slice_multiply_fusion
  701.1 1.6 multiply_subtract_fusion.3
  705.3 2.6 multiply_subtract_fusion.1
  709.7 5.6 add_subtract_fusion
  (495 shorter events, 80.7 us)
Async XLA Ops:
  7.2 14.8 %copy-start = (s32[1,8,512]{2,1,0:T(8,128)S(1)}, s32[1,8,512]{2,1,0:T(8,128)}, u32[]{:S(2)}) copy-start(s32[1,8,512]{2,1,0:T(8,128)} %param.37) | copy-start | bytes 49156
  7.2 91.8 %all-gather.9.cloned.1.call-start = ((), (), s32[]{:S(2)}) async-start(), calls=%async_computation.8 | async-start | bytes 1536000 | tf_op jit(solution)/shard_map/all_gather | solution.py:511
  11.3 94.9 %all-gather.5.cloned.1.call-start = ((), (), s32[]{:S(2)}) async-start(), calls=%async_computation.6 | async-start | bytes 4663296 | tf_op jit(solution)/shard_map/all_gather | solution.py:495
  12.2 150.4 %all-gather.7.cloned.1.call-start = ((), (), s32[]{:S(2)}) async-start(), calls=%async_computation.7 | async-start | bytes 2433024 | tf_op jit(solution)/shard_map/all_gather | solution.py:496
  12.9 223.3 %all-gather.11.cloned.1.call-start = ((), (), s32[]{:S(2)}) async-start(), calls=%async_computation.9 | async-start | bytes 7372800 | tf_op jit(solution)/shard_map/all_gather | solution.py:512
  18.0 440.6 %reduce-scatter.9.cloned.1.call-start = ((), (), s32[]{:S(2)}) async-start(), calls=%async_computation.10 | async-start | bytes 1536000 | tf_op jit(solution)/shard_map/reduce_scatter | solution.py:779
  27.7 67.3 %copy-start.98 = (s32[512]{0:T(512)}, s32[512]{0:T(512)S(1)}, u32[]{:S(2)}) copy-start(s32[512]{0:T(512)S(1)} %get-tuple-element.713) | copy-start | bytes 6148
  82.6 10.7 %copy-start.97 = (s32[1,1,512]{2,1,0:T(1,128)S(1)}, s32[1,1,512]{2,1,0:T(1,128)}, u32[]{:S(2)}) copy-start(s32[1,1,512]{2,1,0:T(1,128)} %param.38) | copy-start | bytes 6148
  82.6 10.6 %copy-start.137 = (s32[1,1,64]{2,1,0:T(1,128)S(1)}, s32[1,1,64]{2,1,0:T(1,128)}, u32[]{:S(2)}) copy-start(s32[1,1,64]{2,1,0:T(1,128)} %param.39) | copy-start | bytes 772
  82.7 10.9 %copy-start.18 = (bf16[4,8,80,192]{3,2,1,0:T(8,128)(2,1)S(1)}, bf16[4,8,80,192]{3,2,1,0:T(8,128)(2,1)}, u32[]{:S(2)}) copy-start(bf16[4,8,80,192]{3,2,1,0:T(8,128)(2,1)} %get-tuple-element.296) | copy-start | bytes 2949124
  108.1 7.7 %copy-start.67 = (f32[512]{0:T(512)}, f32[512]{0:T(512)S(1)}, u32[]{:S(2)}) copy-start(f32[512]{0:T(512)S(1)} %broadcast_multiply_fusion.2) | copy-start | bytes 6148
  127.8 34.7 %copy-start.54 = (f32[768]{0:T(1024)S(1)}, f32[768]{0:T(1024)}, u32[]{:S(2)}) copy-start(f32[768]{0:T(1024)} %mul.1103) | copy-start | bytes 9220
  129.7 35.4 %copy-start.60 = (f32[768]{0:T(1024)S(1)}, f32[768]{0:T(1024)}, u32[]{:S(2)}) copy-start(f32[768]{0:T(1024)} %get-tuple-element.581) | copy-start | bytes 9220
  162.5 21.7 %copy-start.9 = (bf16[4,192,384]{2,1,0:T(8,128)(2,1)S(1)}, bf16[4,192,384]{2,1,0:T(8,128)(2,1)}, u32[]{:S(2)}) copy-start(bf16[4,192,384]{2,1,0:T(8,128)(2,1)} %get-tuple-element.696) | copy-start | bytes 1769476
  162.5 21.7 %copy-start.123 = (f32[384]{0:T(512)S(1)}, f32[384]{0:T(512)}, u32[]{:S(2)}) copy-start(f32[384]{0:T(512)} %reshape.765) | copy-start | bytes 4612
  164.3 46.1 %copy-start.78 = (f32[64]{0:T(128)}, f32[64]{0:T(128)S(1)}, u32[]{:S(2)}) copy-start(f32[64]{0:T(128)S(1)} %broadcast_multiply_fusion.7) | copy-start | bytes 772
  164.6 45.9 %copy-start.82 = (f32[64]{0:T(128)}, f32[64]{0:T(128)S(1)}, u32[]{:S(2)}) copy-start(f32[64]{0:T(128)S(1)} %fusion.209) | copy-start | bytes 772
  165.8 20.1 %copy-start.33 = (bf16[4,192,384]{2,1,0:T(8,128)(2,1)S(1)}, bf16[4,192,384]{2,1,0:T(8,128)(2,1)}, u32[]{:S(2)}) copy-start(bf16[4,192,384]{2,1,0:T(8,128)(2,1)} %get-tuple-element.695) | copy-start | bytes 1769476
  165.8 20.1 %copy-start.120 = (f32[384]{0:T(512)S(1)}, f32[384]{0:T(512)}, u32[]{:S(2)}) copy-start(f32[384]{0:T(512)} %get-tuple-element.672) | copy-start | bytes 4612
  186.0 24.5 %copy-start.58 = (f32[768]{0:T(1024)S(1)}, f32[768]{0:T(1024)}, u32[]{:S(2)}) copy-start(f32[768]{0:T(1024)} %get-tuple-element.580) | copy-start | bytes 9220
  186.0 26.4 %copy-start.28 = (bf16[768,1536]{1,0:T(8,128)(2,1)S(1)}, bf16[768,1536]{1,0:T(8,128)(2,1)}, u32[]{:S(2)}) copy-start(bf16[768,1536]{1,0:T(8,128)(2,1)} %all-gather.7.cloned.1.call-done) | copy-start | bytes 7077892
  187.6 24.8 %copy-start.55 = (f32[768]{0:T(1024)S(1)}, f32[768]{0:T(1024)}, u32[]{:S(2)}) copy-start(f32[768]{0:T(1024)} %get-tuple-element.579) | copy-start | bytes 9220
  187.6 24.8 %copy-start.75 = (f32[768]{0:T(1024)S(1)}, f32[768]{0:T(1024)}, u32[]{:S(2)}) copy-start(f32[768]{0:T(1024)} %get-tuple-element.578) | copy-start | bytes 9220
  187.6 24.8 %copy-start.114 = (f32[768]{0:T(1024)S(1)}, f32[768]{0:T(1024)}, u32[]{:S(2)}) copy-start(f32[768]{0:T(1024)} %get-tuple-element.577) | copy-start | bytes 9220
  236.2 6.1 slice-start
  271.0 8.2 %copy-start.8 = (bf16[512,3840]{1,0:T(8,128)(2,1)}, bf16[512,3840]{1,0:T(8,128)(2,1)S(1)}, u32[]{:S(2)}) copy-start(bf16[512,3840]{1,0:T(8,128)(2,1)S(1)} %get-tuple-element.654) | copy-start | bytes 11796484
  271.0 24.4 %copy-start.85 = (f32[64]{0:T(128)S(1)}, f32[64]{0:T(128)}, u32[]{:S(2)}) copy-start(f32[64]{0:T(128)} %copy-done.84) | copy-start | bytes 772
  271.0 24.4 %copy-start.107 = (f32[64]{0:T(128)S(1)}, f32[64]{0:T(128)}, u32[]{:S(2)}) copy-start(f32[64]{0:T(128)} %copy-done.106) | copy-start | bytes 772
  271.0 26.1 %copy-start.132 = (f32[64]{0:T(128)S(1)}, f32[64]{0:T(128)}, u32[]{:S(2)}) copy-start(f32[64]{0:T(128)} %copy-done.131) | copy-start | bytes 772
  279.3 19.9 %copy-start.29 = (bf16[768,1536]{1,0:T(8,128)(2,1)S(1)}, bf16[768,1536]{1,0:T(8,128)(2,1)}, u32[]{:S(2)}) copy-start(bf16[768,1536]{1,0:T(8,128)(2,1)} %all-gather.7.cloned.1.call-done) | copy-start | bytes 7077892
  279.3 19.9 %copy-start.56 = (f32[768]{0:T(1024)S(1)}, f32[768]{0:T(1024)}, u32[]{:S(2)}) copy-start(f32[768]{0:T(1024)} %get-tuple-element.579) | copy-start | bytes 9220
  279.3 19.9 %copy-start.102 = (f32[64]{0:T(128)S(1)}, f32[64]{0:T(128)}, u32[]{:S(2)}) copy-start(f32[64]{0:T(128)} %copy-done.101) | copy-start | bytes 772
  279.3 19.9 %copy-start.116 = (f32[64]{0:T(128)S(1)}, f32[64]{0:T(128)}, u32[]{:S(2)}) copy-start(f32[64]{0:T(128)} %copy-done.115) | copy-start | bytes 772
  299.1 23.8 %copy-start.38 = (bf16[64,768]{1,0:T(8,128)(2,1)}, bf16[64,768]{1,0:T(8,128)(2,1)S(1)}, u32[]{:S(2)}) copy-start(bf16[64,768]{1,0:T(8,128)(2,1)S(1)} %get-tuple-element.660) | copy-start | bytes 294916
  299.2 23.8 %copy-start.34 = (bf16[4,192,384]{2,1,0:T(8,128)(2,1)S(1)}, bf16[4,192,384]{2,1,0:T(8,128)(2,1)}, u32[]{:S(2)}) copy-start(bf16[4,192,384]{2,1,0:T(8,128)(2,1)} %get-tuple-element.695) | copy-start | bytes 1769476
  299.2 23.8 %copy-start.121 = (f32[384]{0:T(512)S(1)}, f32[384]{0:T(512)}, u32[]{:S(2)}) copy-start(f32[384]{0:T(512)} %get-tuple-element.672) | copy-start | bytes 4612
  299.2 23.8 %copy-start.145 = (f32[512,384]{1,0:T(8,128)S(1)}, f32[512,384]{1,0:T(8,128)}, u32[]{:S(2)}) copy-start(f32[512,384]{1,0:T(8,128)} %copy-done.144) | copy-start | bytes 2359300
  300.5 22.5 %copy-start.118 = (f32[64]{0:T(128)}, f32[64]{0:T(128)S(1)}, u32[]{:S(2)}) copy-start(f32[64]{0:T(128)S(1)} %negate_multiply_fusion.2) | copy-start | bytes 772
  335.2 21.5 %copy-start.79 = (f32[64]{0:T(128)S(1)}, f32[64]{0:T(128)}, u32[]{:S(2)}) copy-start(f32[64]{0:T(128)} %copy-done.78) | copy-start | bytes 772
  335.2 21.5 %copy-start.83 = (f32[64]{0:T(128)S(1)}, f32[64]{0:T(128)}, u32[]{:S(2)}) copy-start(f32[64]{0:T(128)} %copy-done.82) | copy-start | bytes 772
  335.2 21.5 %copy-start.119 = (f32[64]{0:T(128)S(1)}, f32[64]{0:T(128)}, u32[]{:S(2)}) copy-start(f32[64]{0:T(128)} %copy-done.118) | copy-start | bytes 772
  335.2 23.3 %copy-start.128 = (f32[64]{0:T(128)S(1)}, f32[64]{0:T(128)}, u32[]{:S(2)}) copy-start(f32[64]{0:T(128)} %copy-done.127) | copy-start | bytes 772
  335.3 159.9 %reduce-scatter.13.cloned.1.call-start = ((), (), s32[]{:S(2)}) async-start(), calls=%async_computation.12 | async-start | bytes 2433024
  335.3 23.4 %copy-start.30 = (bf16[768,1536]{1,0:T(8,128)(2,1)S(1)}, bf16[768,1536]{1,0:T(8,128)(2,1)}, u32[]{:S(2)}) copy-start(bf16[768,1536]{1,0:T(8,128)(2,1)} %all-gather.7.cloned.1.call-done) | copy-start | bytes 7077892
  360.1 7.1 copy-start.44
  373.0 228.9 %reduce-scatter.15.cloned.1.call-start = ((), (), s32[]{:S(2)}) async-start(), calls=%async_computation.13 | async-start | bytes 4663296
  394.4 265.0 %reduce-scatter.11.cloned.1.call-start = ((), (), s32[]{:S(2)}) async-start(), calls=%async_computation.11 | async-start | bytes 7372800 | tf_op jit(solution)/shard_map/reduce_scatter | solution.py:720
  402.8 13.0 %copy-start.108 = (f32[768]{0:T(1024)S(1)}, f32[768]{0:T(1024)}, u32[]{:S(2)}) copy-start(f32[768]{0:T(1024)} %get-tuple-element.699) | copy-start | bytes 9220
  421.9 36.7 %copy-start.140 = (f32[12]{0:T(128)S(1)}, f32[12]{0:T(128)}, u32[]{:S(2)}) copy-start(f32[12]{0:T(128)} %get-tuple-element.656) | copy-start | bytes 148
  421.9 36.7 %copy-start.139 = (f32[12]{0:T(128)S(1)}, f32[12]{0:T(128)}, u32[]{:S(2)}) copy-start(f32[12]{0:T(128)} %get-tuple-element.715) | copy-start | bytes 148
  459.5 143.8 %copy-start.110 = (f32[2,96]{1,0:T(2,128)}, f32[2,96]{1,0:T(2,128)S(1)}, u32[]{:S(2)}) copy-start(f32[2,96]{1,0:T(2,128)S(1)} %scatter-add.20) | copy-start | bytes 2308
  605.3 54.1 %copy-start.35 = (f32[24,512]{1,0:T(8,128)}, f32[24,512]{1,0:T(8,128)S(1)}, u32[]{:S(2)}) copy-start(f32[24,512]{1,0:T(8,128)S(1)} %copy.416) | copy-start | bytes 147460
  605.6 53.7 %copy-start.12 = (f32[24,2304]{1,0:T(8,128)}, f32[24,2304]{1,0:T(8,128)S(1)}, u32[]{:S(2)}) copy-start(f32[24,2304]{1,0:T(8,128)S(1)} %copy.414) | copy-start | bytes 663556
  605.9 64.1 %copy-start.48 = (f32[14,24]{1,0:T(8,128)}, f32[14,24]{1,0:T(8,128)S(1)}, u32[]{:S(2)}) copy-start(f32[14,24]{1,0:T(8,128)S(1)} %scatter-add.19) | copy-start | bytes 4036
  677.3 26.7 %copy-start.49 = (f32[14,24]{1,0:T(8,128)S(1)}, f32[14,24]{1,0:T(8,128)}, u32[]{:S(2)}) copy-start(f32[14,24]{1,0:T(8,128)} %copy-done.48) | copy-start | bytes 4036
  677.3 26.7 %copy-start.64 = (f32[14,24]{1,0:T(8,128)S(1)}, f32[14,24]{1,0:T(8,128)}, u32[]{:S(2)}) copy-start(f32[14,24]{1,0:T(8,128)} %param.48) | copy-start | bytes 4036
  700.3 8.2 %copy-start.10 = (f32[2,192,384]{2,1,0:T(8,128)S(1)}, f32[2,192,384]{2,1,0:T(8,128)}, u32[]{:S(2)}) copy-start(f32[2,192,384]{2,1,0:T(8,128)} %param.51) | copy-start | bytes 1769476
  701.0 6.9 copy-start.126
  701.0 6.9 copy-start.134
  701.0 6.9 copy-start.135
  701.0 6.9 copy-start.136
  701.0 7.4 %copy-start.11 = (f32[1,384,384]{2,1,0:T(8,128)S(1)}, f32[1,384,384]{2,1,0:T(8,128)}, u32[]{:S(2)}) copy-start(f32[1,384,384]{2,1,0:T(8,128)} %slice_multiply_fusion) | copy-start | bytes 1769476
  701.0 7.4 %copy-start.31 = (f32[2,192,384]{2,1,0:T(8,128)S(1)}, f32[2,192,384]{2,1,0:T(8,128)}, u32[]{:S(2)}) copy-start(f32[2,192,384]{2,1,0:T(8,128)} %param.53) | copy-start | bytes 1769476
  701.1 7.4 %copy-start.32 = (f32[2,192,384]{2,1,0:T(8,128)S(1)}, f32[2,192,384]{2,1,0:T(8,128)}, u32[]{:S(2)}) copy-start(f32[2,192,384]{2,1,0:T(8,128)} %param.52) | copy-start | bytes 1769476
  (90 other events, 262.0 us)
Sparse Core Ops, SparseCore 0:
  11.4 20.4 all-gather.8
  34.8 68.7 all-gather.4
  106.5 55.9 all-gather.6
  164.5 43.0 all-gather.10
  335.4 29.3 reduce-scatter.8
  373.2 121.9 reduce-scatter.12
  500.8 101.0 reduce-scatter.14
  604.7 54.6 reduce-scatter.10
